TPU v7x, 128 devices: a whole 4x4x4 slice. The times are simulated.
128 devices in a mesh: comp: 2 (over z_lo), tile: 64 (over x, y, z_hi, core).
Axes of the slice: x: 4, y: 4, z: 4 (z_hi: 2, z_lo: 2; z = z_hi * 2 + z_lo), core: 2. Of those that a mesh axis runs over, the one named last changes fastest.
Arguments:
- state: float32 [2, 2, 64, 4096, 256], P('comp', None, None, 'tile'), may hold values from -6 to 6
- horiz_rate: float32 [2, 2, 64], P('comp'), may hold values from 0.02 to 0.2
- vert_rate: float32 [2, 2], P('comp'), may hold values from 0.02 to 0.15
- sea_mask: int32 [4096, 256], P('tile'), may hold values 0 or 1
- exchange_coef: float32 [4096, 256], P('tile'), may hold values from 0.1 to 0.5
- partner: int32 [64], replicated, may hold values from 0 to 63, each once
Outputs:
- new_state: float32 [2, 2, 64, 4096, 256], P('comp', None, None, 'tile')
Inputs may be any that keep to these rules, and one draw needn't show every extreme that they name: `partner`: each tile number appears once.
All inputs are finite; a program needn't handle non-finite values. No bound on the sum of `sea_mask` on one device may be relied on, other than what follows from the above.
Results may differ from a plain program's by a relative error of at most 0.00002.
Values sent between devices are 32-bit elements; how exact they have to be, the bound alone decides.
No kernel may reach another device: no remote copies, remote signals or barrier semaphores. Data moves between devices by JAX's collectives and lax.ppermute only.
A program may use at most 128 MiB of HBM per device.

v0:
```python
import jax
import jax.numpy as jnp
from jax import lax
from jax.sharding import PartitionSpec as P

STEPS = 2


def swapped(value, axis, distance):
    mask = 2**distance
    pairs = [(source, source ^ mask) for source in range(lax.axis_size(axis))]
    return lax.ppermute(value, axis, pairs)


def extended(array, sides, width):
    for axis, dim in sides:
        count, length = (lax.axis_size(axis), array.shape[dim])
        up = [(i, (i + 1) % count) for i in range(count)]
        down = [(j, i) for i, j in up]
        last = lax.slice_in_dim(array, length - width, length, axis=dim)
        initial = lax.slice_in_dim(array, 0, width, axis=dim)
        before = lax.ppermute(last, axis, up)
        after = lax.ppermute(initial, axis, down)
        array = jnp.concatenate([before, array, after], axis=dim)
    return array


def make_picker(target, piece, start):
    count = piece.shape[0]
    offset = jnp.clip(target, 0, count - 1)
    picked = lax.dynamic_index_in_dim(piece, offset, 0, keepdims=False)
    inside = jnp.logical_and(target >= start, target < start + count)
    return jnp.where(inside, picked, jnp.zeros_like(picked))


def per_device(state, horiz_rate, vert_rate, sea_mask, exchange_coef, partner):
    comp_index = lax.axis_index("comp")
    tile_index = lax.axis_index("tile")
    ntile = lax.axis_size("tile")
    is_atmos = comp_index == 0
    fields = state[0]
    seaf = sea_mask.astype(jnp.float32)
    plane_two = jnp.where(is_atmos, exchange_coef, seaf)
    outgoing = jnp.stack([fields[0, 0], plane_two])
    order = jnp.arange(ntile, dtype=jnp.int32)
    inverse = jnp.sum(jnp.where(partner[None, :] == order[:, None], order[None, :], 0), axis=1)
    across = swapped(outgoing, "comp", 0)
    source = jnp.where(is_atmos, partner[tile_index], inverse[tile_index])
    theirs = make_picker(
        source, lax.all_gather(across[None], "tile", axis=0, tiled=True), jnp.int32(0)
    )
    atm_surf = jnp.where(is_atmos, outgoing[0], theirs[0])
    ocn_surf = jnp.where(is_atmos, theirs[0], outgoing[0])
    coef = jnp.where(is_atmos, outgoing[1], theirs[1])
    wet = jnp.where(is_atmos, theirs[1], outgoing[1])
    flux = coef * (atm_surf - ocn_surf) * wet
    surface = jnp.where(is_atmos, atm_surf - flux, ocn_surf + flux)
    fields = fields.at[0, 0].set(surface)
    horiz = horiz_rate[0]
    vert = vert_rate[0]
    scale = jnp.where(is_atmos, jnp.ones_like(seaf), seaf)
    for step in range(STEPS):
        padded = extended(fields, (("tile", 2),), 1)
        lap = (
            padded[:, :, 2:]
            + padded[:, :, :-2]
            + jnp.roll(fields, 1, -1)
            + jnp.roll(fields, -1, -1)
            - 4.0 * fields
        )
        above = jnp.concatenate([fields[:, 1:], fields[:, -1:]], 1)
        below = jnp.concatenate([fields[:, :1], fields[:, :-1]], 1)
        vlap = above + below - 2.0 * fields
        fields = fields + horiz[:, :, None, None] * lap + vert[:, None, None, None] * vlap
        fields = fields * scale
    return fields[None]


def solution(mesh):
    placed = (
        P("comp", None, None, "tile", None),
        P("comp", None, None),
        P("comp", None),
        P("tile", None),
        P("tile", None),
        P(),
    )
    return jax.shard_map(
        per_device,
        mesh=mesh,
        in_specs=placed,
        out_specs=P("comp", None, None, "tile", None),
        check_vma=False,
    )
```

profile of v0, /device:TPU:0, one launch (start us, length us, event | category | flops | bytes accessed | tf_op | source)
XLA Modules:
  0.0 220.2 jit_solution(5615533458879213191)
XLA Ops:
  6.5 7.9 %copy.9 = f32[1,2,64,64,256]{4,3,2,1,0:T(8,128)} copy(f32[1,2,64,64,256]{4,3,2,1,0:T(8,128)} %param.8) | data formatting | bytes 16777216
  14.5 0.8 slice_bitcast_fusion.1
  15.4 2.1 collective-permute-start
  17.5 3.5 %collective-permute-done = f32[2,64,256]{2,1,0:T(8,128)S(1)} collective-permute-done((f32[2,64,256]{2,1,0:T(8,128)S(1)}, f32[2,64,256]{2,1,0:T(8,128)S(1)}, u32[]{:S(2)}, u32[]{:S(2)}) %collective-permute-start) | collective-permute-done | bytes 131104 | tf_op jit(solution)/shard_map/ppermute | solution.py:12
  21.0 0.7 copy-done.2
  21.7 0.7 dynamic_slice.10
  24.3 83.4 %all-gather.3.cloned.1.call-done = f32[128,64,256]{2,1,0:T(8,128)} async-done(((f32[2,64,256]{2,1,0:T(8,128)}), f32[128,64,256]{2,1,0:T(8,128)}) %all-gather.3.cloned.1.call-update) | async-done | bytes 8388624 | tf_op jit(solution)/shard_map/all_gather | solution.py:50
  107.7 0.9 dynamic-slice_select_fusion
  108.6 0.7 bitcast_dynamic-update-slice_fusion
  109.2 1.9 fusion.34
  111.1 7.1 %fusion.33 = (f32[2,64,64,1]{3,2,1,0:T(8,128)S(1)}, f32[2,64,64,1]{3,2,1,0:T(8,128)}) fusion(f32[2,64,64,256]{3,2,1,0:T(8,128)} %bitcast_dynamic-update-slice_fusion), kind=kLoop, calls=%fused_computation.51 | loop fusion | bytes 131072 | tf_op jit(solution)/shard_map/jit(_roll_static)/slice | solution.py:68
  118.2 6.2 %fusion.31 = (f32[2,63,64,256]{3,2,1,0:T(8,128)}, f32[2,63,64,256]{3,2,1,0:T(8,128)}) fusion(f32[2,64,64,256]{3,2,1,0:T(8,128)S(1)} %bitcast.41), kind=kLoop, calls=%fused_computation.49 | loop fusion | bytes 33030144 | tf_op jit(solution)/shard_map/slice | solution.py:72
  124.5 7.4 %fusion.32 = (f32[2,64,64,255]{3,2,1,0:T(8,128)}, f32[2,64,64,255]{3,2,1,0:T(8,128)}) fusion(f32[2,64,64,256]{3,2,1,0:T(8,128)S(1)} %bitcast.41), kind=kLoop, calls=%fused_computation.50 | loop fusion | bytes 33423360 | tf_op jit(solution)/shard_map/jit(_roll_static)/slice | solution.py:68
  131.9 2.4 %collective-permute-start.1 = (f32[2,64,1,256]{3,2,1,0:T(1,128)S(1)}, f32[2,64,1,256]{3,2,1,0:T(1,128)S(1)}, u32[]{:S(2)}, u32[]{:S(2)}) collective-permute-start(f32[2,64,1,256]{3,2,1,0:T(1,128)S(1)} %get-tuple-element.35), channel_id=1, source_target_pairs={{1,0},{2,1},{3,2},{4,3},{5,4},{6,5},{7,6},{8,7},{9,8},{10,9},{11,1... | collective-permute-start | bytes 393224 | tf_op jit(solution)/shard_map/ppermute | solution.py:23
  134.3 2.5 %collective-permute-done.1 = f32[2,64,1,256]{3,2,1,0:T(1,128)S(1)} collective-permute-done((f32[2,64,1,256]{3,2,1,0:T(1,128)S(1)}, f32[2,64,1,256]{3,2,1,0:T(1,128)S(1)}, u32[]{:S(2)}, u32[]{:S(2)}) %collective-permute-start.1) | collective-permute-done | bytes 131104 | tf_op jit(solution)/shard_map/ppermute | solution.py:23
  136.8 7.6 %collective-permute-done.2 = f32[2,64,1,256]{3,2,1,0:T(1,128)S(1)} collective-permute-done((f32[2,64,1,256]{3,2,1,0:T(1,128)S(1)}, f32[2,64,1,256]{3,2,1,0:T(1,128)S(1)}, u32[]{:S(2)}, u32[]{:S(2)}) %collective-permute-start.2) | collective-permute-done | bytes 131104 | tf_op jit(solution)/shard_map/ppermute | solution.py:22
  144.4 18.2 %fusion.16 = f32[2,64,64,256]{3,2,1,0:T(8,128)} fusion(f32[2,64,64,256]{3,2,1,0:T(8,128)S(1)} %bitcast.41, f32[2,64,1,256]{3,2,1,0:T(1,128)S(1)} %collective-permute-done.2, f32[2,64,1,256]{3,2,1,0:T(1,128)S(1)} %collective-permute-done.1, f32[2,64,64,255]{3,2,1,0:T(8,128)} %get-tuple-element.32, f32[2,64,64,1]{3,2,1,0:T(8,128)} %get-tuple-element.34, ...), kind=kLoop, calls=%fused_computation.19 | loop fusion | flops 39845888 | bytes 50659848 | tf_op jit(solution)/shard_map/mul | solution.py:75
  162.6 1.9 fusion.29
  164.5 7.1 %fusion.28 = (f32[2,64,64,1]{3,2,1,0:T(8,128)S(1)}, f32[2,64,64,1]{3,2,1,0:T(8,128)}) fusion(f32[2,64,64,256]{3,2,1,0:T(8,128)} %fusion.16), kind=kLoop, calls=%fused_computation.46 | loop fusion | bytes 131072 | tf_op jit(solution)/shard_map/jit(_roll_static)/slice | solution.py:68
  171.6 6.2 %fusion.26 = (f32[2,63,64,256]{3,2,1,0:T(8,128)}, f32[2,63,64,256]{3,2,1,0:T(8,128)}) fusion(f32[2,64,64,256]{3,2,1,0:T(8,128)S(1)} %bitcast.43), kind=kLoop, calls=%fused_computation.44 | loop fusion | bytes 33030144 | tf_op jit(solution)/shard_map/slice | solution.py:72
  177.8 7.2 %fusion.27 = (f32[2,64,64,255]{3,2,1,0:T(8,128)}, f32[2,64,64,255]{3,2,1,0:T(8,128)}) fusion(f32[2,64,64,256]{3,2,1,0:T(8,128)S(1)} %bitcast.43), kind=kLoop, calls=%fused_computation.45 | loop fusion | bytes 33423360 | tf_op jit(solution)/shard_map/jit(_roll_static)/slice | solution.py:68
  185.6 2.0 collective-permute-done.3
  187.6 7.6 %collective-permute-done.4 = f32[2,64,1,256]{3,2,1,0:T(1,128)S(1)} collective-permute-done((f32[2,64,1,256]{3,2,1,0:T(1,128)S(1)}, f32[2,64,1,256]{3,2,1,0:T(1,128)S(1)}, u32[]{:S(2)}, u32[]{:S(2)}) %collective-permute-start.4) | collective-permute-done | bytes 131104 | tf_op jit(solution)/shard_map/ppermute | solution.py:22
  195.2 18.2 %fusion.8 = f32[1,2,64,64,256]{4,3,2,1,0:T(8,128)} fusion(f32[2,64,64,256]{3,2,1,0:T(8,128)S(1)} %bitcast.43, f32[2,64,1,256]{3,2,1,0:T(1,128)S(1)} %collective-permute-done.4, f32[2,64,1,256]{3,2,1,0:T(1,128)S(1)} %collective-permute-done.3, f32[2,64,64,255]{3,2,1,0:T(8,128)} %get-tuple-element.22, f32[2,64,64,1]{3,2,1,0:T(8,128)} %get-tuple-element.24, ...), kind=kLoop, calls=%fused_computation.9 | loop fusion | flops 39845888 | bytes 50659848 | tf_op jit(solution)/shard_map/broadcast_in_dim | solution.py:76
  (32 shorter events, 1.3 us)
Async XLA Ops:
  6.5 8.8 %copy-start = (s32[64,256]{1,0:T(8,128)S(1)}, s32[64,256]{1,0:T(8,128)}, u32[]{:S(2)}) copy-start(s32[64,256]{1,0:T(8,128)} %param.11) | copy-start | bytes 196612
  6.5 8.8 %copy-start.1 = (f32[64,256]{1,0:T(8,128)S(1)}, f32[64,256]{1,0:T(8,128)}, u32[]{:S(2)}) copy-start(f32[64,256]{1,0:T(8,128)} %param.12) | copy-start | bytes 196612
  6.5 15.1 %copy-start.5 = (s32[64]{0:T(128)S(1)}, s32[64]{0:T(128)}, u32[]{:S(2)}) copy-start(s32[64]{0:T(128)} %param.13) | copy-start | bytes 772
  6.5 101.1 %all-gather.3.cloned.1.call-start = ((), (), s32[]{:S(2)}) async-start(), calls=%async_computation | async-start | bytes 8519680 | tf_op jit(solution)/shard_map/all_gather | solution.py:50
  15.4 5.6 %collective-permute-start = (f32[2,64,256]{2,1,0:T(8,128)S(1)}, f32[2,64,256]{2,1,0:T(8,128)S(1)}, u32[]{:S(2)}, u32[]{:S(2)}) collective-permute-start(f32[2,64,256]{2,1,0:T(8,128)S(1)} %pad_maximum_fusion.4), channel_id=1, source_target_pairs={{0,64},{64,0},{1,65},{65,1},{2,66},{66,2},{3,67},{67,3},{4,68},{68... | collective-permute-start | bytes 393224 | tf_op jit(solution)/shard_map/ppermute | solution.py:12
  21.0 0.7 copy-start.2
  109.2 9.0 %slice-start = ((s8[8388608]{0:T(1024)(128)(4,1)}), s8[4194304]{0:T(1024)(128)(4,1)S(1)}, s32[]{:S(2)}) async-start(s8[8388608]{0:T(1024)(128)(4,1)} %bitcast.40), calls=%async_computation.1 | async-start | bytes 8388608
  111.1 7.1 %slice-start.1 = ((s8[8388608]{0:T(1024)(128)(4,1)}), s8[4194304]{0:T(1024)(128)(4,1)S(1)}, s32[]{:S(2)}) async-start(s8[8388608]{0:T(1024)(128)(4,1)} %bitcast.40), calls=%async_computation.2 | async-start | bytes 8388608
  124.5 19.9 %copy-start.3 = (f32[1,2,64]{2,1,0:T(2,128)S(1)}, f32[1,2,64]{2,1,0:T(2,128)}, u32[]{:S(2)}) copy-start(f32[1,2,64]{2,1,0:T(2,128)} %param.9) | copy-start | bytes 1540
  124.5 19.9 %copy-start.4 = (f32[1,2]{1,0:T(1,128)S(1)}, f32[1,2]{1,0:T(1,128)}, u32[]{:S(2)}) copy-start(f32[1,2]{1,0:T(1,128)} %param.10) | copy-start | bytes 28
  131.9 4.9 %collective-permute-start.1 = (f32[2,64,1,256]{3,2,1,0:T(1,128)S(1)}, f32[2,64,1,256]{3,2,1,0:T(1,128)S(1)}, u32[]{:S(2)}, u32[]{:S(2)}) collective-permute-start(f32[2,64,1,256]{3,2,1,0:T(1,128)S(1)} %get-tuple-element.35), channel_id=1, source_target_pairs={{1,0},{2,1},{3,2},{4,3},{5,4},{6,5},{7,6},{8,7},{9,8},{10,9},{11,1... | collective-permute-start | bytes 393224 | tf_op jit(solution)/shard_map/ppermute | solution.py:23
  134.2 10.1 %collective-permute-start.2 = (f32[2,64,1,256]{3,2,1,0:T(1,128)S(1)}, f32[2,64,1,256]{3,2,1,0:T(1,128)S(1)}, u32[]{:S(2)}, u32[]{:S(2)}) collective-permute-start(f32[2,64,1,256]{3,2,1,0:T(1,128)S(1)} %get-tuple-element.36), channel_id=1, source_target_pairs={{0,1},{1,2},{2,3},{3,4},{4,5},{5,6},{6,7},{7,8},{8,9},{9,10},{10,1... | collective-permute-start | bytes 393224 | tf_op jit(solution)/shard_map/ppermute | solution.py:22
  162.6 9.0 %slice-start.2 = ((s8[8388608]{0:T(1024)(128)(4,1)}), s8[4194304]{0:T(1024)(128)(4,1)S(1)}, s32[]{:S(2)}) async-start(s8[8388608]{0:T(1024)(128)(4,1)} %bitcast.42), calls=%async_computation.3 | async-start | bytes 8388608
  164.5 7.1 %slice-start.3 = ((s8[8388608]{0:T(1024)(128)(4,1)}), s8[4194304]{0:T(1024)(128)(4,1)S(1)}, s32[]{:S(2)}) async-start(s8[8388608]{0:T(1024)(128)(4,1)} %bitcast.42), calls=%async_computation.4 | async-start | bytes 8388608
  185.1 2.5 %collective-permute-start.3 = (f32[2,64,1,256]{3,2,1,0:T(1,128)S(1)}, f32[2,64,1,256]{3,2,1,0:T(1,128)S(1)}, u32[]{:S(2)}, u32[]{:S(2)}) collective-permute-start(f32[2,64,1,256]{3,2,1,0:T(1,128)S(1)} %get-tuple-element.25), channel_id=1, source_target_pairs={{1,0},{2,1},{3,2},{4,3},{5,4},{6,5},{7,6},{8,7},{9,8},{10,9},{11,1... | collective-permute-start | bytes 393224 | tf_op jit(solution)/shard_map/ppermute | solution.py:23
  185.1 10.1 %collective-permute-start.4 = (f32[2,64,1,256]{3,2,1,0:T(1,128)S(1)}, f32[2,64,1,256]{3,2,1,0:T(1,128)S(1)}, u32[]{:S(2)}, u32[]{:S(2)}) collective-permute-start(f32[2,64,1,256]{3,2,1,0:T(1,128)S(1)} %get-tuple-element.26), channel_id=1, source_target_pairs={{0,1},{1,2},{2,3},{3,4},{4,5},{5,6},{6,7},{7,8},{8,9},{9,10},{10,1... | collective-permute-start | bytes 393224 | tf_op jit(solution)/shard_map/ppermute | solution.py:22
Sparse Core Ops, SparseCore 0:
  21.8 85.8 all-gather.2
where the time goes:
time: 220 us
  waiting for transfers between devices  107 us (49%)
  local copies, waits for them, and re-layouts  55.8 us (25%)
  other arithmetic  38.1 us (17%)
  between operations  14.7 us (7%)
  starting transfers between devices  4.97 us (2%)
    all_gather x1, waiting for transfers between devices, per_device(): lax.all_gather(across[None], 'tile', axis=0, tiled=True)  83.4 us
    slice x4, local copies, waits for them, and re-layouts, per_device(): jnp.roll(fields, -1, -1)  28.8 us
    mul x1, other arithmetic, per_device(): fields = fields * scale  18.2 us
    broadcast_in_dim x1, other arithmetic, per_device(): return fields[None]  18.2 us
    ppermute x2, waiting for transfers between devices, extended(): before = lax.ppermute(last, axis, up)  15.2 us
    slice x4, local copies, waits for them, and re-layouts, per_device(): below = jnp.concatenate([fields[:, :1], fields[:, :-1]], 1)  12.5 us
    unnamed x21, local copies, waits for them, and re-layouts  8.62 us
    ppermute x2, waiting for transfers between devices, extended(): after = lax.ppermute(initial, axis, down)  4.51 us
  transfers between devices with their start and end apart: 6, of which 6 were waited for; matrix products, arithmetic and copies ran while one was open for 1% of the time, Pallas kernels for 0%

commit v1 on v0

v1 whole, which is shorter than its diff:
```python
import functools

import jax
import jax.numpy as jnp
from jax import lax
from jax.experimental import pallas as pl
from jax.experimental.pallas import tpu as pltpu
from jax.sharding import PartitionSpec as P

BOTH = ("comp", "tile")
CHUNK = 8
MIB = 1 << 20


def row_ids(rows, width):
    return lax.broadcasted_iota(jnp.int32, (rows, width), 0)


def beside(x):
    width = x.shape[-1]
    return pltpu.roll(x, 1, 1) + pltpu.roll(x, width - 1, 1)


def around(groups, before, after, top, bottom):
    down = [pltpu.roll(x, 1, 0) for x in groups]
    up = [pltpu.roll(x, 7, 0) for x in groups]
    down_edge = [jnp.broadcast_to(before, groups[0].shape)] + down[:-1]
    up_edge = up[1:] + [jnp.broadcast_to(after, groups[0].shape)]
    return [
        (jnp.where(top, de, d) + jnp.where(bottom, ue, u)) + beside(x)
        for x, d, de, u, ue in zip(groups, down, down_edge, up, up_edge)
    ]


def mix_kernel(hz, vt, state, mine_first, mine_last, before, after, mask, hcol, dep, out, base, raw, s1, res, edge, in_sem, out_sem):
    del dep
    fields, levels, rows, width = state.shape
    per = levels // CHUNK
    total = fields * per

    def load(q):
        f, c = q // per, q % per
        where = (f, pl.ds(c * CHUNK, CHUNK))
        return pltpu.make_async_copy(state.at[where], raw.at[where], in_sem.at[q])

    def store(q):
        f, c = q // per, q % per
        where = (f, pl.ds(c * CHUNK, CHUNK))
        return pltpu.make_async_copy(res.at[where], out.at[where], out_sem.at[q])

    @pl.loop(0, total)
    def _(q):
        load(q).start()

    planes = fields * levels
    level = row_ids(levels, width)
    for side, (x2, x1, x0, m) in enumerate(
        (
            (before.at[0], before.at[1], mine_first.at[0], before[1, planes : planes + 1, :]),
            (after.at[1], after.at[0], mine_last.at[1], after[0, planes : planes + 1, :]),
        )
    ):
        for f in range(fields):
            at = pl.ds(f * levels, levels)
            x = x1[at, :]
            lap = x2[at, :] + x0[at, :] + beside(x)
            below = jnp.where(level == 0, x, pltpu.roll(x, 1, 0))
            above = jnp.where(level == levels - 1, x, pltpu.roll(x, levels - 1, 0))
            h = hcol[at, :]
            v = vt[f]
            new = x * (1.0 - 4.0 * h - 2.0 * v) + h * lap + v * (above + below)
            edge[side, at, :] = new * m

    row = row_ids(8, width)
    top, bottom = row == 0, row == 7
    ngroups = rows // 8

    def split(ref, f, l):
        return [ref[f, l, pl.ds(8 * g, 8), :] for g in range(ngroups)]

    def substep(src, dst, f, l, ahead, behind):
        h, v = hz[f, l], vt[f]
        c0 = 1.0 - 4.0 * h - 2.0 * v
        lo, hi = jnp.maximum(l - 1, 0), jnp.minimum(l + 1, levels - 1)
        x = split(src, f, l)
        p = f * levels + l
        lap = around(x, ahead[pl.ds(p, 1), :], behind[pl.ds(p, 1), :], top, bottom)
        for g in range(ngroups):
            at = pl.ds(8 * g, 8)
            vert = src[f, lo, at, :] + src[f, hi, at, :]
            dst[f, l, at, :] = (x[g] * c0 + h * lap[g] + v * vert) * mask[at, :]

    def first(f, l):
        substep(raw, s1, f, l, before.at[1], after.at[0])

    def second(f, l):
        substep(s1, res, f, l, edge.at[0], edge.at[1])

    @pl.loop(0, total)
    def _(q):
        f, c = q // per, q % per

        @pl.when(c == 0)
        def _():
            load(q).wait()
            first(f, 0)

        @pl.when(c < per - 1)
        def _():
            load(q + 1).wait()

        @pl.loop(0, CHUNK, unroll=2)
        def _(i):
            l = c * CHUNK + i
            first(f, jnp.minimum(l + 1, levels - 1))
            second(f, l)

        store(q).start()

        @pl.when(q == 0)
        def _():
            base[...] = res[0, 0:3]

    @pl.loop(0, total)
    def _(q):
        store(q).wait()


def mix(fields, hz, vt, first, last, before, after, mask, dep):
    nf, levels, rows, width = fields.shape
    planes = nf * levels
    vmem = pl.BlockSpec(memory_space=pltpu.VMEM)
    smem = pl.BlockSpec(memory_space=pltpu.SMEM)
    anyw = pl.BlockSpec(memory_space=pl.ANY)
    total = nf * levels // CHUNK
    return pl.pallas_call(
        mix_kernel,
        out_shape=(
            jax.ShapeDtypeStruct(fields.shape, jnp.float32),
            jax.ShapeDtypeStruct((3, rows, width), jnp.float32),
        ),
        in_specs=[smem, smem, anyw, vmem, vmem, vmem, vmem, vmem, vmem, anyw],
        out_specs=(anyw, vmem),
        scratch_shapes=[
            pltpu.VMEM(fields.shape, jnp.float32),
            pltpu.VMEM(fields.shape, jnp.float32),
            pltpu.VMEM(fields.shape, jnp.float32),
            pltpu.VMEM((2, planes, width), jnp.float32),
            pltpu.SemaphoreType.DMA((total,)),
            pltpu.SemaphoreType.DMA((total,)),
        ],
        compiler_params=pltpu.CompilerParams(vmem_limit_bytes=40 * MIB),
        cost_estimate=pl.CostEstimate(flops=26 * fields.size, bytes_accessed=8 * fields.size, transcendentals=0),
        name="mix",
    )(hz, vt, fields, first, last, before, after, mask, hz.reshape(planes, 1), dep)


def flux_kernel(partner, place, got, back, theirs, turned):
    tiles = got.shape[0] // 2
    half = got.shape[1] // 2
    for t in range(tiles):
        theirs[t : t + 1, :] = got[pl.ds(tiles + partner[t], 1), :]
    flux = got[0:tiles, half:] * (got[0:tiles, 0:half] - theirs[:, 0:half]) * theirs[:, half:]
    back[0:tiles, 0:half] = flux
    for t in range(tiles):
        turned[pl.ds(partner[t], 1), :] = back[t : t + 1, 0:half]
    other = turned[...]
    back[tiles:, 0:half] = other
    near_start = place[0] < 2

    @pl.when(near_start)
    def _():
        back[0:tiles, half:] = pltpu.roll(flux, tiles - 1, 0)
        back[tiles:, half:] = pltpu.roll(other, tiles - 1, 0)

    @pl.when(jnp.logical_not(near_start))
    def _():
        back[0:tiles, half:] = pltpu.roll(flux, 1, 0)
        back[tiles:, half:] = pltpu.roll(other, 1, 0)


def flux_pieces(partner, place, got):
    vmem = pl.BlockSpec(memory_space=pltpu.VMEM)
    smem = pl.BlockSpec(memory_space=pltpu.SMEM)
    tiles, half = got.shape[0] // 2, got.shape[1] // 2
    return pl.pallas_call(
        flux_kernel,
        out_shape=jax.ShapeDtypeStruct(got.shape, jnp.float32),
        in_specs=[smem, smem, vmem],
        out_specs=vmem,
        scratch_shapes=[pltpu.VMEM((tiles, 2 * half), jnp.float32), pltpu.VMEM((tiles, half), jnp.float32)],
        cost_estimate=pl.CostEstimate(flops=4 * got.size, bytes_accessed=8 * got.size, transcendentals=0),
        name="flux",
    )(partner, place, got)


def add_kernel(hz, vt, sign, base, back, mask, medge, whole, out, ext, three, sem):
    del whole
    rows, width = mask.shape
    half = width // 2
    v, s = vt[0], sign[0]
    zero_pad = jnp.zeros((8, width), jnp.float32)
    ext[0:8, :] = zero_pad
    ext[8 + rows : 16 + rows, :] = zero_pad
    for k in range(2):
        lanes = pl.ds(k * half, half)
        ext[8 : 8 + rows, lanes] = back[pl.ds(k * rows, rows), 0:half] * s
        ext[6:8, lanes] = back[pl.ds(k * rows + rows - 2, 2), half:] * s
        ext[8 + rows : 10 + rows, lanes] = back[pl.ds(k * rows, 2), half:] * s

    total = rows + 16
    m = jnp.concatenate(
        [jnp.broadcast_to(medge[0:1, :], (8, width)), mask[...], jnp.broadcast_to(medge[1:2, :], (8, width))], 0
    )

    def lateral(x):
        return pltpu.roll(x, 1, 0) + pltpu.roll(x, total - 1, 0) + beside(x)

    d = ext[...]
    h0, h1 = hz[0, 0], hz[0, 1]
    one0 = m * ((1.0 - 4.0 * h0 - v) * d + h0 * lateral(d))
    one1 = m * (v * d)
    two0 = (1.0 - 4.0 * h0 - v) * one0 + h0 * lateral(one0) + v * one1
    two1 = (1.0 - 4.0 * h1 - 2.0 * v) * one1 + h1 * lateral(one1) + v * one0
    two2 = v * one1
    for level, two in enumerate((two0, two1, two2)):
        three[level] = base[level] + (m * two)[8 : 8 + rows]
    copy = pltpu.make_async_copy(three, out.at[0, pl.ds(0, 3)], sem)
    copy.start()
    copy.wait()


def add_flux(hz, vt, sign, base, back, mask, medge, whole):
    vmem = pl.BlockSpec(memory_space=pltpu.VMEM)
    smem = pl.BlockSpec(memory_space=pltpu.SMEM)
    anyw = pl.BlockSpec(memory_space=pl.ANY)
    rows, width = mask.shape
    return pl.pallas_call(
        add_kernel,
        out_shape=jax.ShapeDtypeStruct(whole.shape, jnp.float32),
        in_specs=[smem, smem, smem, vmem, vmem, vmem, vmem, anyw],
        out_specs=anyw,
        scratch_shapes=[pltpu.VMEM((rows + 16, width), jnp.float32), pltpu.VMEM(base.shape, jnp.float32), pltpu.SemaphoreType.DMA],
        input_output_aliases={7: 0},
        cost_estimate=pl.CostEstimate(flops=30 * mask.size, bytes_accessed=32 * mask.size, transcendentals=0),
        name="add",
    )(hz, vt, sign, base, back, mask, medge, whole)


def halves(plane):
    half = plane.shape[1] // 2
    return jnp.concatenate([plane[:, :half], plane[:, half:]], 0)


def edge_rows(fields, scale, start):
    nf, levels, _, width = fields.shape
    rows = lax.slice_in_dim(fields, start, start + 2, axis=2).transpose(2, 0, 1, 3).reshape(2, nf * levels, width)
    return jnp.concatenate([rows, scale[start : start + 2][:, None]], 1)


def per_device(state, horiz_rate, vert_rate, sea_mask, exchange_coef, partner):
    is_atmos = lax.axis_index("comp") == 0
    ntile = lax.axis_size("tile")
    fields, hz, vt = state[0], horiz_rate[0], vert_rate[0]
    rows = fields.shape[2]
    wet = sea_mask.astype(jnp.float32)
    scale = jnp.where(is_atmos, jnp.ones_like(wet), wet)

    outgoing = jnp.concatenate([halves(fields[0, 0]), halves(jnp.where(is_atmos, exchange_coef, wet))], 1)
    got = lax.all_to_all(outgoing, BOTH, 0, 0, tiled=True)
    place = lax.axis_index("tile").astype(jnp.int32).reshape(1)
    pieces = flux_pieces(partner, place, got)
    back = lax.all_to_all(pieces, BOTH, 0, 0, tiled=True)

    up = [(i, (i + 1) % ntile) for i in range(ntile)]
    down = [(j, i) for i, j in up]
    first, last = edge_rows(fields, scale, 0), edge_rows(fields, scale, rows - 2)
    before, after = lax.ppermute(last, "tile", up), lax.ppermute(first, "tile", down)

    whole, base = mix(fields, hz, vt, first, last, before, after, scale, pieces)
    medge = jnp.concatenate([before[1, -1:], after[0, -1:]], 0)
    sign = jnp.where(is_atmos, -1.0, 1.0).astype(jnp.float32).reshape(1)
    return add_flux(hz, vt, sign, base, back, scale, medge, whole)[None]


def solution(mesh):
    placed = (
        P("comp", None, None, "tile", None),
        P("comp", None, None),
        P("comp", None),
        P("tile", None),
        P("tile", None),
        P(),
    )
    return jax.shard_map(
        per_device,
        mesh=mesh,
        in_specs=placed,
        out_specs=P("comp", None, None, "tile", None),
        check_vma=False,
    )
```

time: 220 us -> 72.2 us (0.33)
  waiting for transfers between devices: 107 us -> 9.88 us
  local copies, waits for them, and re-layouts: 55.8 us -> 13.7 us
  other arithmetic: 38.1 us -> 1.48 us
  Pallas kernels: 0 us -> 23.3 us
  starting transfers between devices: 4.97 us -> 23.3 us
  between operations: 14.7 us -> 0.15 us
    all_gather x1 -> x0, waiting for transfers between devices: 83.4 us -> none  [per_device(): lax.all_gather(across[None], 'tile', axis=0, tiled=True)]
    slice x10 -> x2, local copies, waits for them, and re-layouts: 45.1 us -> 1.75 us  [the longest x1 1.74 us: edge_rows(): lax.slice_in_dim(fields, start, start + 2, axis=2).transpose(2, 0, 1, 3)]
    pallas_call x0 -> x3, Pallas kernels: none -> 23.3 us  [the longest x1 19.6 us: mix(): pl.pallas_call(mix_kernel, out_shape=(jax.ShapeDtypeStruct(fields.shape,...]
    ppermute x5 -> x2, waiting for transfers between devices: 23.2 us -> 1.39 us  [the longest x1 1.39 us: per_device(): lax.ppermute(first, 'tile', down)]
    mul x1 -> x0, other arithmetic: 18.2 us -> none  [per_device(): fields = fields * scale]
    broadcast_in_dim x1 -> x0, other arithmetic: 18.2 us -> none  [per_device(): return fields[None]]
    all_to_all x0 -> x2, starting transfers between devices: none -> 16.1 us  [the longest x1 11.1 us: per_device(): got = lax.all_to_all(outgoing, BOTH, 0, 0, tiled=True)]
    all_to_all x0 -> x2, waiting for transfers between devices: none -> 8.49 us  [the longest x1 7.31 us: per_device(): got = lax.all_to_all(outgoing, BOTH, 0, 0, tiled=True)]
  transfers between devices with their start and end apart: 6 -> 4, of which waited for: 6 -> 3; matrix products, arithmetic and copies ran while one was open for 1% -> 8% of each run, Pallas kernels for 0% -> 2%
where the time goes in v1:
time: 72.2 us; the launch traced here: 71.8 us
  starting transfers between devices  23.3 us (32%)
  Pallas kernels  23.3 us (32%)
  local copies, waits for them, and re-layouts  13.7 us (19%)
  waiting for transfers between devices  9.88 us (14%)
  other arithmetic  1.48 us (2%)
    pallas_call x1, Pallas kernels, mix(): pl.pallas_call(mix_kernel, out_shape=(jax.ShapeDtypeStruct(fields.shape,...  19.6 us
    all_to_all x1, starting transfers between devices, per_device(): got = lax.all_to_all(outgoing, BOTH, 0, 0, tiled=True)  11.1 us
    unnamed x16, local copies, waits for them, and re-layouts  7.67 us
    all_to_all x1, waiting for transfers between devices, per_device(): got = lax.all_to_all(outgoing, BOTH, 0, 0, tiled=True)  7.31 us
    ppermute x1, starting transfers between devices, per_device(): lax.ppermute(first, 'tile', down)  7.15 us
    all_to_all x1, starting transfers between devices, per_device(): back = lax.all_to_all(pieces, BOTH, 0, 0, tiled=True)  4.95 us
    pallas_call x1, Pallas kernels, add_flux(): pl.pallas_call(add_kernel, out_shape=jax.ShapeDtypeStruct(whole.shape, jn...  1.95 us
    pallas_call x1, Pallas kernels, flux_pieces(): pl.pallas_call(flux_kernel, out_shape=jax.ShapeDtypeStruct(got.shape, jnp...  1.75 us
  transfers between devices with their start and end apart: 4, of which 3 were waited for; matrix products, arithmetic and copies ran while one was open for 8% of the time, Pallas kernels for 2%

profile of v1, /device:TPU:0, one launch (start us, length us, event | category | flops | bytes accessed | tf_op | source)
XLA Modules:
  0.0 71.8 jit_solution(6307084490569236244)
XLA Ops:
  0.0 0.8 %slice_bitcast_fusion = f32[64,256]{1,0:T(8,128)S(1)} fusion(f32[2,64,64,256]{3,2,1,0:T(8,128)} %bitcast.31), kind=kLoop, calls=%fused_computation.5 | loop fusion | bytes 131072 | tf_op jit(solution)/shard_map/squeeze | solution.py:269
  0.8 0.9 %convert_select_fusion = (f32[64,256]{1,0:T(8,128)S(1)}, f32[64,256]{1,0:T(8,128)S(1)}) fusion(f32[64,256]{1,0:T(8,128)} %param.10, s32[64,256]{1,0:T(8,128)} %param.9, pred[]{:T(512)S(6)} %eq.3), kind=kLoop, calls=%fused_computation.6 | loop fusion | flops 49152 | bytes 262145 | tf_op jit(solution)/shard_map/jit(_where)/select_n | solution.py:269
  1.8 0.8 %copy.17 = f32[128,1,256]{2,1,0:T(1,128)} copy(f32[128,1,256]{2,0,1:T(8,128)S(1)} %maximum_bitcast_fusion) | data formatting | bytes 262144 | tf_op jit(solution)/shard_map/all_to_all | solution.py:270
  2.6 11.1 %all-to-all-start = ((f32[128,1,256]{2,1,0:T(1,128)}), f32[128,1,256]{2,1,0:T(1,128)S(1)}, u32[]{:S(2)}, u32[]{:S(2)}) async-start(f32[128,1,256]{2,1,0:T(1,128)} %copy.17), calls=%async_computation | async-start | bytes 262144 | tf_op jit(solution)/shard_map/all_to_all | solution.py:270
  13.7 1.7 %fusion = (f32[2,64,2,256]{3,2,1,0:T(2,128)S(1)}, f32[2,64,2,256]{3,2,1,0:T(2,128)S(1)}) fusion(f32[2,64,64,256]{3,2,1,0:T(8,128)} %bitcast.32), kind=kLoop, calls=%fused_computation.13 | loop fusion | bytes 1048576 | tf_op jit(solution)/shard_map/slice | solution.py:257
  15.5 0.1 collective-permute-start
  15.6 7.3 %all-to-all-done = f32[128,1,256]{2,1,0:T(1,128)S(1)} async-done(((f32[128,1,256]{2,1,0:T(1,128)}), f32[128,1,256]{2,1,0:T(1,128)S(1)}, u32[]{:S(2)}, u32[]{:S(2)}) %all-to-all-start) | async-done | bytes 131104 | tf_op jit(solution)/shard_map/all_to_all | solution.py:270
  22.9 0.7 copy.27
  23.6 1.8 %flux.1.dep = f32[128,256]{1,0:T(8,128)} custom-call(s32[64]{0:T(128)} %partner.1, s32[1]{0:T(128)} %bitcast.10.place, f32[128,256]{1,0:T(8,128)} %bitcast.42), custom_call_target="tpu_custom_call" | custom-call | flops 131072 | bytes 262144 | tf_op jit(solution)/shard_map/flux/pallas_call | solution.py:186
  25.3 1.7 %copy.19 = f32[128,1,256]{2,1,0:T(1,128)} copy(f32[128,1,256]{2,0,1:T(8,128)} %bitcast.34) | data formatting | bytes 262144 | tf_op jit(solution)/shard_map/all_to_all | solution.py:273
  27.0 5.0 %all-to-all-start.1 = ((f32[128,1,256]{2,1,0:T(1,128)}), f32[128,1,256]{2,1,0:T(1,128)S(1)}, u32[]{:S(2)}, u32[]{:S(2)}) async-start(f32[128,1,256]{2,1,0:T(1,128)} %copy.19), calls=%async_computation.1 | async-start | bytes 262144 | tf_op jit(solution)/shard_map/all_to_all | solution.py:273
  32.1 7.1 %collective-permute-start.1 = (f32[2,129,256]{2,1,0:T(8,128)S(1)}, f32[2,129,256]{2,1,0:T(8,128)S(1)}, u32[]{:S(2)}, u32[]{:S(2)}) collective-permute-start(f32[2,129,256]{2,1,0:T(8,128)S(1)} %dynamic-update-slice.3.mine_first), channel_id=1, source_target_pairs={{1,0},{2,1},{3,2},{4,3},{5,4},{6,5},{7,6},{8,7},{9,8},{10,9},{11,1... | collective-permute-start | bytes 792584 | tf_op jit(solution)/shard_map/ppermute | solution.py:278
  39.2 0.8 %reshape_squeeze.4.hcol = f32[128,1]{1,0:T(8,128)S(1)} reshape(f32[1,2,64]{2,1,0:T(2,128)} %param.7) | data formatting | bytes 1024 | tf_op jit(solution)/shard_map/reshape;squeeze | solution.py:155
  40.1 1.2 %all-to-all-done.1 = f32[128,1,256]{2,1,0:T(1,128)S(1)} async-done(((f32[128,1,256]{2,1,0:T(1,128)}), f32[128,1,256]{2,1,0:T(1,128)S(1)}, u32[]{:S(2)}, u32[]{:S(2)}) %all-to-all-start.1) | async-done | bytes 131104 | tf_op jit(solution)/shard_map/all_to_all | solution.py:273
  41.2 0.7 copy.26
  41.9 1.4 %collective-permute-done.1.after = f32[2,129,256]{2,1,0:T(8,128)S(1)} collective-permute-done((f32[2,129,256]{2,1,0:T(8,128)S(1)}, f32[2,129,256]{2,1,0:T(8,128)S(1)}, u32[]{:S(2)}, u32[]{:S(2)}) %collective-permute-start.1) | collective-permute-done | bytes 264224 | tf_op jit(solution)/shard_map/ppermute | solution.py:278
  43.3 0.6 pad_maximum_fusion.medge
  43.9 3.4 %copy-done = f32[1,2,64,64,256]{4,3,2,1,0:T(8,128)S(1)} copy-done((f32[1,2,64,64,256]{4,3,2,1,0:T(8,128)S(1)}, f32[1,2,64,64,256]{4,3,2,1,0:T(8,128)}, u32[]{:S(2)}) %copy-start) | copy-done | bytes 8388632
  47.3 0.9 %copy-done.1 = f32[128,256]{1,0:T(8,128)S(1)} copy-done((f32[128,256]{1,0:T(8,128)S(1)}, f32[128,256]{1,0:T(8,128)}, u32[]{:S(2)}) %copy-start.1) | copy-done | bytes 131096
  48.2 0.7 copy-done.4
  48.9 0.7 copy-done.5
  49.5 19.6 %mix.1 = (f32[2,64,64,256]{3,2,1,0:T(8,128)}, f32[3,64,256]{2,1,0:T(8,128)S(1)}) custom-call(f32[2,64]{1,0:T(2,128)S(1)} %bitcast.36, f32[2]{0:T(128)S(1)} %bitcast.38, f32[2,64,64,256]{3,2,1,0:T(8,128)S(1)} %bitcast.33, f32[2,129,256]{2,1,0:T(8,128)S(1)} %dynamic-update-slice.3.mine_first, f32[2,129,256]{2,1,0:T(8,128)S(1)} %dynamic-update-slice.1.mine_last, ...), custom_call_target="tpu_custom_call" | custom-call | flops 54525952 | bytes 16777216 | tf_op jit(solution)/shard_map/mix/pallas_call | solution.py:136
  69.1 0.7 copy-done.3
  69.8 1.9 %add.1 = f32[2,64,64,256]{3,2,1,0:T(8,128)} custom-call(f32[2,64]{1,0:T(2,128)} %bitcast.35, f32[2]{0:T(128)} %bitcast.37, f32[1]{0:T(128)} %bitcast.2.sign, f32[3,64,256]{2,1,0:T(8,128)} %copy-done.3, f32[128,256]{1,0:T(8,128)} %bitcast.41, f32[64,256]{1,0:T(8,128)} %copy-done.2, f32[2,256]{1,0:T(2,128)} %pad_maximum_fusion.medge, ...), custom_call_target="tpu_custom_call", output_to_operand_aliasing={{}: (7, {})} | custom-call | flops 491520 | bytes 524288 | tf_op jit(solution)/shard_map/add/pallas_call | solution.py:238
  (19 shorter events, 0.2 us)
Async XLA Ops:
  1.7 68.1 %copy-start.2 = (f32[64,256]{1,0:T(8,128)}, f32[64,256]{1,0:T(8,128)S(1)}, u32[]{:S(2)}) copy-start(f32[64,256]{1,0:T(8,128)S(1)} %get-tuple-element.16.mask) | copy-start | bytes 196612
  2.6 20.4 %all-to-all-start = ((f32[128,1,256]{2,1,0:T(1,128)}), f32[128,1,256]{2,1,0:T(1,128)S(1)}, u32[]{:S(2)}, u32[]{:S(2)}) async-start(f32[128,1,256]{2,1,0:T(1,128)} %copy.17), calls=%async_computation | async-start | bytes 262144 | tf_op jit(solution)/shard_map/all_to_all | solution.py:270
  15.5 26.4 %collective-permute-start = (f32[2,129,256]{2,1,0:T(8,128)S(1)}, f32[2,129,256]{2,1,0:T(8,128)S(1)}, u32[]{:S(2)}, u32[]{:S(2)}) collective-permute-start(f32[2,129,256]{2,1,0:T(8,128)S(1)} %dynamic-update-slice.1.mine_last), channel_id=1, source_target_pairs={{0,1},{1,2},{2,3},{3,4},{4,5},{5,6},{6,7},{7,8},{8,9},{9,10},{10,1... | collective-permute-start | bytes 792584 | tf_op jit(solution)/shard_map/ppermute | solution.py:278
  27.0 14.2 %all-to-all-start.1 = ((f32[128,1,256]{2,1,0:T(1,128)}), f32[128,1,256]{2,1,0:T(1,128)S(1)}, u32[]{:S(2)}, u32[]{:S(2)}) async-start(f32[128,1,256]{2,1,0:T(1,128)} %copy.19), calls=%async_computation.1 | async-start | bytes 262144 | tf_op jit(solution)/shard_map/all_to_all | solution.py:273
  32.1 11.2 %collective-permute-start.1 = (f32[2,129,256]{2,1,0:T(8,128)S(1)}, f32[2,129,256]{2,1,0:T(8,128)S(1)}, u32[]{:S(2)}, u32[]{:S(2)}) collective-permute-start(f32[2,129,256]{2,1,0:T(8,128)S(1)} %dynamic-update-slice.3.mine_first), channel_id=1, source_target_pairs={{1,0},{2,1},{3,2},{4,3},{5,4},{6,5},{7,6},{8,7},{9,8},{10,9},{11,1... | collective-permute-start | bytes 792584 | tf_op jit(solution)/shard_map/ppermute | solution.py:278
  43.9 3.4 %copy-start = (f32[1,2,64,64,256]{4,3,2,1,0:T(8,128)S(1)}, f32[1,2,64,64,256]{4,3,2,1,0:T(8,128)}, u32[]{:S(2)}) copy-start(f32[1,2,64,64,256]{4,3,2,1,0:T(8,128)} %param.6) | copy-start | bytes 25165828
  47.3 0.9 %copy-start.1 = (f32[128,256]{1,0:T(8,128)S(1)}, f32[128,256]{1,0:T(8,128)}, u32[]{:S(2)}) copy-start(f32[128,256]{1,0:T(8,128)} %flux.1.dep) | copy-start | bytes 393220
  48.2 0.7 copy-start.4
  48.9 0.7 copy-start.5
  69.1 0.7 copy-start.3

commit v2 on v1

v2 whole, which is shorter than its diff:
```python
import functools

import jax
import jax.numpy as jnp
from jax import lax
from jax.experimental import pallas as pl
from jax.experimental.pallas import tpu as pltpu
from jax.sharding import PartitionSpec as P

BOTH = ("comp", "tile")
CHUNK = 8
UNROLL = 8
MIB = 1 << 20


def row_ids(rows, width):
    return lax.broadcasted_iota(jnp.int32, (rows, width), 0)


def beside(x):
    half = x.shape[-1] // 2
    a, b = x[:, :half], x[:, half:]
    lane = lax.broadcasted_iota(jnp.int32, a.shape, 1)
    first, last = lane == 0, lane == half - 1
    ra, rb = pltpu.roll(a, 1, 1), pltpu.roll(b, 1, 1)
    la, lb = pltpu.roll(a, half - 1, 1), pltpu.roll(b, half - 1, 1)
    left = jnp.where(first, rb, ra) + jnp.where(last, lb, la)
    right = jnp.where(first, ra, rb) + jnp.where(last, la, lb)
    return jnp.concatenate([left, right], 1)


def mix_kernel(
    place, hz_any, vt_any, state, sent_near, sent_far, got_near, got_far, mask, out, base, aux,
    mine, halo, strip_sem, hz, vt, hcol, raw, s1, res, edge, split, wet, rate_sem, in_sem, out_sem,
):
    fields, levels, rows, width = state.shape
    per = levels // CHUNK
    total = fields * per
    half = width // 2
    sides = [pl.ds(k * half, half) for k in range(2)]

    def load(q):
        f, c = q // per, q % per
        where = (f, pl.ds(c * CHUNK, CHUNK))
        return [
            pltpu.make_async_copy(state.at[(*where, slice(None), lanes)], raw.at[(k, *where)], in_sem.at[q, k])
            for k, lanes in enumerate(sides)
        ]

    def store(q):
        f, c = q // per, q % per
        where = (f, pl.ds(c * CHUNK, CHUNK))
        return [
            pltpu.make_async_copy(res.at[(k, *where)], out.at[(*where, slice(None), lanes)], out_sem.at[q, k])
            for k, lanes in enumerate(sides)
        ]

    @pl.loop(0, total)
    def _(q):
        for copy in load(q):
            copy.start()

    odd = place[0] % 2
    strips = [
        pltpu.make_async_copy(src, dst.at[slot], strip_sem.at[i])
        for i, (src, dst, slot) in enumerate(
            ((sent_near, mine, 1 - odd), (sent_far, mine, odd), (got_near, halo, 1 - odd), (got_far, halo, odd))
        )
    ]
    for copy in strips:
        copy.start()
    planes = fields * levels
    rates = [pltpu.make_async_copy(hz_any, hz, rate_sem.at[0]), pltpu.make_async_copy(vt_any, vt, rate_sem.at[1])]
    for copy in rates:
        copy.start()
    for copy in rates:
        copy.wait()

    for p in range(planes):
        hcol[p : p + 1, :] = jnp.full((1, half), hz[p // levels, p % levels], jnp.float32)

    for copy in strips:
        copy.wait()
    mine_first, mine_last, before, after = mine.at[0], mine.at[1], halo.at[0], halo.at[1]
    for j in range(4):
        aux[j : j + 1, :] = jnp.full((1, width), (hz[0, 0], hz[0, 1], vt[0], vt[0])[j], jnp.float32)
    aux[4:5, :] = before[1, planes : planes + 1, :]
    aux[5:6, :] = after[0, planes : planes + 1, :]

    level = row_ids(levels, width)
    for side, (x2, x1, x0, m) in enumerate(
        (
            (before.at[0], before.at[1], mine_first.at[0], before[1, planes : planes + 1, :]),
            (after.at[1], after.at[0], mine_last.at[1], after[0, planes : planes + 1, :]),
        )
    ):
        for f in range(fields):
            at = pl.ds(f * levels, levels)
            x = x1[at, :]
            lap = x2[at, :] + x0[at, :] + beside(x)
            below = jnp.where(level == 0, x, pltpu.roll(x, 1, 0))
            above = jnp.where(level == levels - 1, x, pltpu.roll(x, levels - 1, 0))
            h = jnp.concatenate([hcol[at, :]] * 2, 1)
            v = vt[f]
            new = x * (1.0 - 4.0 * h - 2.0 * v) + h * lap + v * (above + below)
            edge[side, at, :] = new * m

    row = row_ids(8, width)
    top, bottom = row == 0, row == 7
    nrow = rows // 8

    def spread(ref, f, l, r):
        return jnp.concatenate([ref[k, f, l, pl.ds(r, 8, stride=nrow), :] for k in range(2)], 1)

    def packed(ref, f, l, r):
        return ref[f, l, pl.ds(8 * r, 8), :]

    for k, lanes in enumerate(sides):
        split[k] = mask[:, lanes]
        for r in range(nrow):
            wet[pl.ds(8 * r, 8), lanes] = split[k, pl.ds(r, 8, stride=nrow), :]

    def substep(get, src, f, l, ahead, behind):
        h, v = hz[f, l], vt[f]
        c0 = 1.0 - 4.0 * h - 2.0 * v
        lo, hi = jnp.maximum(l - 1, 0), jnp.minimum(l + 1, levels - 1)
        p = f * levels + l
        x = [get(src, f, l, r) for r in range(nrow)]
        above = jnp.where(top, jnp.broadcast_to(ahead[pl.ds(p, 1), :], (8, width)), pltpu.roll(x[-1], 1, 0))
        under = jnp.where(bottom, jnp.broadcast_to(behind[pl.ds(p, 1), :], (8, width)), pltpu.roll(x[0], 7, 0))
        for r in range(nrow):
            near = (x[r - 1] if r else above) + (x[r + 1] if r < nrow - 1 else under)
            vert = get(src, f, lo, r) + get(src, f, hi, r)
            new = x[r] * c0 + h * (near + beside(x[r])) + v * vert
            yield r, new * wet[pl.ds(8 * r, 8), :]

    def first(f, l):
        for r, new in substep(spread, raw, f, l, before.at[1], after.at[0]):
            s1[f, l, pl.ds(8 * r, 8), :] = new

    def second(f, l):
        for r, new in substep(packed, s1, f, l, edge.at[0], edge.at[1]):
            for k, lanes in enumerate(sides):
                res[k, f, l, pl.ds(r, 8, stride=nrow), :] = new[:, k * half : (k + 1) * half]

    for copy in load(0):
        copy.wait()

    @pl.loop(0, total + 1)
    def _(q):
        @pl.when(q < total - 1)
        def _():
            for copy in load(q + 1):
                copy.wait()

        @pl.when(q < total)
        def _():
            @pl.loop(0, CHUNK, unroll=UNROLL)
            def _(i):
                first(q // per, (q % per) * CHUNK + i)

        @pl.when(q > 0)
        def _():
            @pl.loop(0, CHUNK, unroll=UNROLL)
            def _(i):
                second((q - 1) // per, ((q - 1) % per) * CHUNK + i)

            for copy in store(q - 1):
                copy.start()

        @pl.when(q == 1)
        def _():
            for k, lanes in enumerate(sides):
                base[:, :, lanes] = res[k, 0, 0:3]

    @pl.loop(0, total)
    def _(q):
        for copy in store(q):
            copy.wait()


def mix(place, fields, hz, vt, sent_near, sent_far, got_near, got_far, mask):
    nf, levels, rows, width = fields.shape
    planes = nf * levels
    vmem = pl.BlockSpec(memory_space=pltpu.VMEM)
    smem = pl.BlockSpec(memory_space=pltpu.SMEM)
    anyw = pl.BlockSpec(memory_space=pl.ANY)
    hbm = pl.BlockSpec(memory_space=pltpu.HBM)
    total = nf * levels // CHUNK
    halved = (2, nf, levels, rows, width // 2)
    return pl.pallas_call(
        mix_kernel,
        out_shape=(
            jax.ShapeDtypeStruct(fields.shape, jnp.float32),
            jax.ShapeDtypeStruct((3, rows, width), jnp.float32),
            jax.ShapeDtypeStruct((8, width), jnp.float32),
        ),
        in_specs=[smem, hbm, hbm, hbm, anyw, anyw, anyw, anyw, vmem],
        out_specs=(hbm, vmem, vmem),
        scratch_shapes=[
            pltpu.VMEM((2, 2, planes + 8, width), jnp.float32),
            pltpu.VMEM((2, 2, planes + 8, width), jnp.float32),
            pltpu.SemaphoreType.DMA((4,)),
            pltpu.SMEM((nf, levels), jnp.float32),
            pltpu.SMEM((nf,), jnp.float32),
            pltpu.VMEM((planes, width // 2), jnp.float32),
            pltpu.VMEM(halved, jnp.float32),
            pltpu.VMEM(fields.shape, jnp.float32),
            pltpu.VMEM(halved, jnp.float32),
            pltpu.VMEM((2, planes, width), jnp.float32),
            pltpu.VMEM((2, rows, width // 2), jnp.float32),
            pltpu.VMEM((rows, width), jnp.float32),
            pltpu.SemaphoreType.DMA((2,)),
            pltpu.SemaphoreType.DMA((total, 2)),
            pltpu.SemaphoreType.DMA((total, 2)),
        ],
        compiler_params=pltpu.CompilerParams(vmem_limit_bytes=46 * MIB),
        cost_estimate=pl.CostEstimate(flops=26 * fields.size, bytes_accessed=8 * fields.size, transcendentals=0),
        name="mix",
    )(place, hz, vt, fields, sent_near, sent_far, got_near, got_far, mask)


def prep_kernel(atmos, state, coef_hbm, sea_hbm, out, wet, surface, coef, sea, sem):
    rows, width = coef.shape
    half = width // 2
    copies = [
        pltpu.make_async_copy(state.at[0, 0], surface, sem.at[0]),
        pltpu.make_async_copy(coef_hbm, coef, sem.at[1]),
        pltpu.make_async_copy(sea_hbm, sea, sem.at[2]),
    ]
    for copy in copies:
        copy.start()
    for copy in copies:
        copy.wait()
    ocean = sea[...].astype(jnp.float32)
    mine = atmos[0] == 1
    second = jnp.where(mine, coef[...], ocean)
    wet[...] = jnp.where(mine, jnp.ones_like(ocean), ocean)
    for k in range(2):
        lanes = slice(k * half, (k + 1) * half)
        out[pl.ds(2 * k * rows, rows, stride=2), :] = surface[:, lanes]
        out[pl.ds(2 * k * rows + 1, rows, stride=2), :] = second[:, lanes]


def prep(atmos, fields, coef, sea):
    smem = pl.BlockSpec(memory_space=pltpu.SMEM)
    vmem = pl.BlockSpec(memory_space=pltpu.VMEM)
    hbm = pl.BlockSpec(memory_space=pltpu.HBM)
    rows, width = coef.shape
    return pl.pallas_call(
        prep_kernel,
        out_shape=(
            jax.ShapeDtypeStruct((4 * rows, width // 2), jnp.float32),
            jax.ShapeDtypeStruct((rows, width), jnp.float32),
        ),
        in_specs=[smem, hbm, hbm, hbm],
        out_specs=(vmem, vmem),
        scratch_shapes=[
            pltpu.VMEM((rows, width), jnp.float32),
            pltpu.VMEM((rows, width), jnp.float32),
            pltpu.VMEM((rows, width), jnp.int32),
            pltpu.SemaphoreType.DMA((3,)),
        ],
        compiler_params=pltpu.CompilerParams(vmem_limit_bytes=60 * MIB),
        cost_estimate=pl.CostEstimate(flops=3 * coef.size, bytes_accessed=24 * coef.size, transcendentals=0),
        name="prep",
    )(atmos, fields, coef, sea)


def edge_kernel(place, atmos, state, sea_any, near, far, stage, sea, sem):
    nf, levels, rows, width = state.shape
    planes = nf * levels
    copies = [
        pltpu.make_async_copy(state.at[:, :, pl.ds(at, 8), :], stage.at[side], sem.at[side])
        for side, at in enumerate((0, rows - 8))
    ]
    copies.append(pltpu.make_async_copy(sea_any, sea, sem.at[2]))
    for copy in copies:
        copy.start()
    for copy in copies:
        copy.wait()

    def fill(first, last):
        for side, (out, at) in enumerate(((first, 0), (last, 6))):
            for j in range(2):
                for f in range(nf):
                    for g in range(0, levels, 8):
                        p = f * levels + g
                        out[j, p : p + 8, :] = stage[side, f, g : g + 8, at + j, :]
                row = side * (rows - 2) + j
                wet = jnp.where(atmos[0] == 1, 1.0, sea[row : row + 1, :].astype(jnp.float32))
                out[j, planes : planes + 8, :] = jnp.broadcast_to(wet, (8, width))

    even = place[0] % 2 == 0

    @pl.when(even)
    def _():
        fill(far, near)

    @pl.when(jnp.logical_not(even))
    def _():
        fill(near, far)


def edges(place, atmos, fields, sea):
    smem = pl.BlockSpec(memory_space=pltpu.SMEM)
    vmem = pl.BlockSpec(memory_space=pltpu.VMEM)
    anyw = pl.BlockSpec(memory_space=pl.ANY)
    hbm = pl.BlockSpec(memory_space=pltpu.HBM)
    nf, levels, _, width = fields.shape
    shape = jax.ShapeDtypeStruct((2, nf * levels + 8, width), jnp.float32)
    return pl.pallas_call(
        edge_kernel,
        out_shape=(shape, shape),
        in_specs=[smem, smem, hbm, anyw],
        out_specs=(vmem, vmem),
        scratch_shapes=[
            pltpu.VMEM((2, nf, levels, 8, width), jnp.float32),
            pltpu.VMEM(sea.shape, jnp.int32),
            pltpu.SemaphoreType.DMA((3,)),
        ],
        compiler_params=pltpu.CompilerParams(vmem_limit_bytes=46 * MIB),
        cost_estimate=pl.CostEstimate(flops=0, bytes_accessed=4 * MIB, transcendentals=0),
        name="edges",
    )(place, atmos, fields, sea)


def flux_kernel(partner, place, got, back, theirs, mine, other):
    tiles = got.shape[0] // 4
    for t in range(tiles):
        theirs[2 * t : 2 * t + 2, :] = got[pl.ds(2 * tiles + 2 * partner[t], 2), :]
    odd, even = pl.ds(1, tiles, stride=2), pl.ds(0, tiles, stride=2)
    flux = got[odd, :] * (got[even, :] - theirs[even, :]) * theirs[odd, :]
    mine[...] = flux
    for t in range(tiles):
        other[pl.ds(partner[t], 1), :] = mine[t : t + 1, :]
    turned = other[...]
    shift = jnp.where(place[0] < 2, tiles - 1, 1)
    back[even, :] = flux
    back[odd, :] = pltpu.roll(flux, shift, 0)
    back[pl.ds(2 * tiles, tiles, stride=2), :] = turned
    back[pl.ds(2 * tiles + 1, tiles, stride=2), :] = pltpu.roll(turned, shift, 0)


def flux_pieces(partner, place, got):
    vmem = pl.BlockSpec(memory_space=pltpu.VMEM)
    smem = pl.BlockSpec(memory_space=pltpu.SMEM)
    tiles, half = got.shape[0] // 4, got.shape[1]
    return pl.pallas_call(
        flux_kernel,
        out_shape=jax.ShapeDtypeStruct(got.shape, jnp.float32),
        in_specs=[smem, smem, vmem],
        out_specs=vmem,
        scratch_shapes=[
            pltpu.VMEM((2 * tiles, half), jnp.float32),
            pltpu.VMEM((tiles, half), jnp.float32),
            pltpu.VMEM((tiles, half), jnp.float32),
        ],
        compiler_params=pltpu.CompilerParams(vmem_limit_bytes=2 * MIB),
        cost_estimate=pl.CostEstimate(flops=10**12, bytes_accessed=8 * got.size, transcendentals=0),
        name="flux",
    )(partner, place, got)


def add_kernel(sign, base, back, mask, aux, whole, out, ext, three, sem):
    del whole
    rows, width = mask.shape
    half = width // 2
    s = sign[0]
    h0, h1, v = (aux[j : j + 1, :] for j in range(3))
    zero_pad = jnp.zeros((8, width), jnp.float32)
    ext[0:8, :] = zero_pad
    ext[8 + rows : 16 + rows, :] = zero_pad
    for k in range(2):
        lanes = pl.ds(k * half, half)
        at = 2 * k * rows
        ext[8 : 8 + rows, lanes] = back[pl.ds(at, rows, stride=2), :] * s
        for j in range(2):
            ext[6 + j : 7 + j, lanes] = back[pl.ds(at + 2 * (rows - 2 + j) + 1, 1), :] * s
            ext[8 + rows + j : 9 + rows + j, lanes] = back[pl.ds(at + 2 * j + 1, 1), :] * s

    total = rows + 16
    m = jnp.concatenate(
        [jnp.broadcast_to(aux[4:5, :], (8, width)), mask[...], jnp.broadcast_to(aux[5:6, :], (8, width))], 0
    )

    def lateral(x):
        return pltpu.roll(x, 1, 0) + pltpu.roll(x, total - 1, 0) + beside(x)

    d = ext[...]
    one0 = m * ((1.0 - 4.0 * h0 - v) * d + h0 * lateral(d))
    one1 = m * (v * d)
    two0 = (1.0 - 4.0 * h0 - v) * one0 + h0 * lateral(one0) + v * one1
    two1 = (1.0 - 4.0 * h1 - 2.0 * v) * one1 + h1 * lateral(one1) + v * one0
    two2 = v * one1
    for level, two in enumerate((two0, two1, two2)):
        three[level] = base[level] + (m * two)[8 : 8 + rows]
    copy = pltpu.make_async_copy(three, out.at[0, pl.ds(0, 3)], sem)
    copy.start()
    copy.wait()


def add_flux(sign, base, back, mask, aux, whole):
    vmem = pl.BlockSpec(memory_space=pltpu.VMEM)
    smem = pl.BlockSpec(memory_space=pltpu.SMEM)
    hbm = pl.BlockSpec(memory_space=pltpu.HBM)
    rows, width = mask.shape
    return pl.pallas_call(
        add_kernel,
        out_shape=jax.ShapeDtypeStruct(whole.shape, jnp.float32),
        in_specs=[smem, vmem, vmem, vmem, vmem, hbm],
        out_specs=hbm,
        scratch_shapes=[pltpu.VMEM((rows + 16, width), jnp.float32), pltpu.VMEM(base.shape, jnp.float32), pltpu.SemaphoreType.DMA],
        input_output_aliases={5: 0},
        compiler_params=pltpu.CompilerParams(vmem_limit_bytes=2 * MIB),
        cost_estimate=pl.CostEstimate(flops=30 * mask.size, bytes_accessed=32 * mask.size, transcendentals=0),
        name="add",
    )(sign, base, back, mask, aux, whole)


def per_device(state, horiz_rate, vert_rate, sea_mask, exchange_coef, partner):
    is_atmos = lax.axis_index("comp") == 0
    ntile = lax.axis_size("tile")
    fields, hz, vt = state[0], horiz_rate[0], vert_rate[0]
    atmos = is_atmos.astype(jnp.int32).reshape(1)
    outgoing, scale = prep(atmos, fields, exchange_coef, sea_mask)
    got = lax.all_to_all(outgoing, BOTH, 0, 0, tiled=True)
    place = lax.axis_index("tile").astype(jnp.int32).reshape(1)
    pieces = flux_pieces(partner, place, got)
    back = lax.all_to_all(pieces, BOTH, 0, 0, tiled=True)

    sent_near, sent_far = edges(place, atmos, fields, sea_mask)
    got_near = lax.ppermute(sent_near, "tile", [(i, i ^ 1) for i in range(ntile)])
    got_far = lax.ppermute(sent_far, "tile", [(i, (i + 2 * (i % 2) - 1) % ntile) for i in range(ntile)])
    whole, base, aux = mix(place, fields, hz, vt, sent_near, sent_far, got_near, got_far, scale)
    sign = jnp.where(is_atmos, -1.0, 1.0).astype(jnp.float32).reshape(1)
    return add_flux(sign, base, back, scale, aux, whole)[None]


def solution(mesh):
    placed = (
        P("comp", None, None, "tile", None),
        P("comp", None, None),
        P("comp", None),
        P("tile", None),
        P("tile", None),
        P(),
    )
    return jax.shard_map(
        per_device,
        mesh=mesh,
        in_specs=placed,
        out_specs=P("comp", None, None, "tile", None),
        check_vma=False,
    )
```

time: 72.2 us -> 48.2 us (0.67)
  local copies, waits for them, and re-layouts: 13.7 us -> 0.02 us
  waiting for transfers between devices: 9.88 us -> 0.01 us
  other arithmetic: 1.48 us -> 0 us
  Pallas kernels: 23.3 us -> 24.3 us
    unnamed x16 -> x10, local copies, waits for them, and re-layouts: 7.67 us -> 0.02 us
    all_to_all x1, waiting for transfers between devices: 7.31 us -> 0.01 us  [per_device(): got = lax.all_to_all(outgoing, BOTH, 0, 0, tiled=True)]
    pallas_call x0 -> x2, Pallas kernels: none -> 4.19 us  [the longest x1 2.55 us: edges(): pl.pallas_call(edge_kernel, out_shape=(shape, shape), in_specs=[smem, sme...]
    all_to_all x2 -> x0, local copies, waits for them, and re-layouts: 2.48 us -> none  [the longest x1 1.69 us: per_device(): back = lax.all_to_all(pieces, BOTH, 0, 0, tiled=True)]
    pallas_call x1, Pallas kernels: 19.6 us -> 17.8 us  [mix(): pl.pallas_call(mix_kernel, out_shape=(jax.ShapeDtypeStruct(fields.shape,...]
    slice x2 -> x0, local copies, waits for them, and re-layouts: 1.75 us -> none  [the longest x1 1.74 us: edge_rows(): lax.slice_in_dim(fields, start, start + 2, axis=2).transpose(2, 0, 1, 3)]
    ppermute x2, waiting for transfers between devices: 1.39 us -> 0.01 us  [the longest x1 0.01 us: per_device(): lax.ppermute(sent_far, 'tile', [(i, (i + 2 * (i % 2) - 1) % ntile) for i...]
    all_to_all x1, waiting for transfers between devices: 1.17 us -> 0.01 us  [per_device(): back = lax.all_to_all(pieces, BOTH, 0, 0, tiled=True)]
  transfers between devices with their start and end apart: 4 -> 4, of which waited for: 3 -> 0; matrix products, arithmetic and copies ran while one was open for 8% -> 0% of each run, Pallas kernels for 2% -> 45%
where the time goes in v2:
time: 48.2 us; the launch traced here: 47.7 us
  Pallas kernels  24.3 us (50%)
  starting transfers between devices  23.3 us (48%)
    pallas_call x1, Pallas kernels, mix(): pl.pallas_call(mix_kernel, out_shape=(jax.ShapeDtypeStruct(fields.shape,...  17.8 us
    all_to_all x1, starting transfers between devices, per_device(): got = lax.all_to_all(outgoing, BOTH, 0, 0, tiled=True)  11.1 us
    ppermute x1, starting transfers between devices, per_device(): lax.ppermute(sent_far, 'tile', [(i, (i + 2 * (i % 2) - 1) % ntile) for i...  7.43 us
    all_to_all x1, starting transfers between devices, per_device(): back = lax.all_to_all(pieces, BOTH, 0, 0, tiled=True)  4.6 us
    pallas_call x1, Pallas kernels, edges(): pl.pallas_call(edge_kernel, out_shape=(shape, shape), in_specs=[smem, sme...  2.55 us
    pallas_call x1, Pallas kernels, prep(): pl.pallas_call(prep_kernel, out_shape=(jax.ShapeDtypeStruct((4 * rows, wi...  1.65 us
    pallas_call x1, Pallas kernels, flux_pieces(): pl.pallas_call(flux_kernel, out_shape=jax.ShapeDtypeStruct(got.shape, jnp...  1.32 us
  transfers between devices with their start and end apart: 4, of which 0 were waited for; matrix products, arithmetic and copies ran while one was open for 0% of the time, Pallas kernels for 45%

profile of v2, /device:TPU:0, one launch (start us, length us, event | category | flops | bytes accessed | tf_op | source)
XLA Modules:
  0.0 47.7 jit_solution(6305565884080131607)
XLA Ops:
  0.0 0.0 copy-start
  0.0 0.0 copy-start.4
  0.0 1.6 %prep.1 = (f32[256,128]{1,0:T(8,128)}, f32[64,256]{1,0:T(8,128)}) custom-call(s32[1]{0:T(128)} %bitcast.5.atmos, f32[2,64,64,256]{3,2,1,0:T(8,128)} %bitcast.15, f32[64,256]{1,0:T(8,128)} %coef_hbm.1, s32[64,256]{1,0:T(8,128)} %sea_hbm.1), custom_call_target="tpu_custom_call" | custom-call | flops 49152 | bytes 393216 | tf_op jit(solution)/shard_map/prep/pallas_call | solution.py:250
  1.7 11.1 %all-to-all-start = ((f32[128,2,128]{2,1,0:T(2,128)}), f32[128,2,128]{2,1,0:T(2,128)S(1)}, u32[]{:S(2)}, u32[]{:S(2)}) async-start(f32[128,2,128]{2,1,0:T(2,128)} %bitcast.18), calls=%async_computation | async-start | bytes 262144 | tf_op jit(solution)/shard_map/all_to_all | solution.py:427
  12.8 0.0 copy-done
  12.8 2.5 %edges.1 = (f32[2,136,256]{2,1,0:T(8,128)}, f32[2,136,256]{2,1,0:T(8,128)}) custom-call(s32[1]{0:T(128)} %bitcast.1.place, s32[1]{0:T(128)} %bitcast.5.atmos, f32[2,64,64,256]{3,2,1,0:T(8,128)} %bitcast.16, s32[64,256]{1,0:T(8,128)S(1)} %copy-done), custom_call_target="tpu_custom_call" | custom-call | bytes 4194304 | tf_op jit(solution)/shard_map/edges/pallas_call | solution.py:312
  15.4 0.1 collective-permute-start
  15.5 7.4 %collective-permute-start.1 = (f32[2,136,256]{2,1,0:T(8,128)}, f32[2,136,256]{2,1,0:T(8,128)}, u32[]{:S(2)}, u32[]{:S(2)}) collective-permute-start(f32[2,136,256]{2,1,0:T(8,128)} %get-tuple-element.13.sent_far), channel_id=1, source_target_pairs={{0,63},{1,2},{2,1},{3,4},{4,3},{5,6},{6,5},{7,8},{8,7},{9,10},{10,... | collective-permute-start | bytes 835592 | tf_op jit(solution)/shard_map/ppermute | solution.py:434
  22.9 0.0 all-to-all-done
  22.9 0.0 copy-done.4
  22.9 0.0 copy-start.1
  22.9 0.0 copy-start.2
  22.9 0.0 copy-start.3
  22.9 1.3 %flux.1 = f32[256,128]{1,0:T(8,128)} custom-call(s32[64]{0:T(128)S(1)} %copy-done.4, s32[1]{0:T(128)} %bitcast.1.place, f32[256,128]{1,0:T(8,128)S(1)} %bitcast.12), custom_call_target="tpu_custom_call" | custom-call | flops 999999995904 | bytes 262144 | tf_op jit(solution)/shard_map/flux/pallas_call | solution.py:349
  24.3 4.6 %all-to-all-start.1 = ((f32[128,2,128]{2,1,0:T(2,128)}), f32[128,2,128]{2,1,0:T(2,128)S(1)}, u32[]{:S(2)}, u32[]{:S(2)}) async-start(f32[128,2,128]{2,1,0:T(2,128)} %bitcast.8), calls=%async_computation.1 | async-start | bytes 262144 | tf_op jit(solution)/shard_map/all_to_all | solution.py:430
  28.9 0.0 collective-permute-done.got_near
  28.9 0.0 collective-permute-done.1.got_far
  28.9 0.0 copy-done.1
  28.9 0.0 copy-done.2
  28.9 0.0 copy-done.3
  28.9 17.8 %mix.1 = (f32[2,64,64,256]{3,2,1,0:T(8,128)}, f32[3,64,256]{2,1,0:T(8,128)S(1)}, f32[8,256]{1,0:T(8,128)S(1)}) custom-call(s32[1]{0:T(128)} %bitcast.1.place, f32[2,64]{1,0:T(2,128)S(1)} %bitcast.13, f32[2]{0:T(128)S(1)} %bitcast.14, f32[2,64,64,256]{3,2,1,0:T(8,128)} %bitcast.17, f32[2,136,256]{2,1,0:T(8,128)} %get-tuple-element.12.sent_near, ...), custom_call_target="tpu_custom_call" | custom-call | flops 54525952 | bytes 16777216 | tf_op jit(solution)/shard_map/mix/pallas_call | solution.py:191
  46.8 0.0 all-to-all-done.1
  46.8 1.0 %add.1 = f32[2,64,64,256]{3,2,1,0:T(8,128)} custom-call(f32[1]{0:T(128)} %bitcast.sign, f32[3,64,256]{2,1,0:T(8,128)S(1)} %get-tuple-element.15.base, f32[256,128]{1,0:T(8,128)S(1)} %bitcast.11, f32[64,256]{1,0:T(8,128)S(1)} %copy-done.1, f32[8,256]{1,0:T(8,128)S(1)} %get-tuple-element.17.aux, ...), custom_call_target="tpu_custom_call", output_to_operand_aliasing={{}: (5, {})} | custom-call | flops 491520 | bytes 524288 | tf_op jit(solution)/shard_map/add/pallas_call | solution.py:408
Async XLA Ops:
  0.0 12.8 %copy-start = (s32[64,256]{1,0:T(8,128)S(1)}, s32[64,256]{1,0:T(8,128)}, u32[]{:S(2)}) copy-start(s32[64,256]{1,0:T(8,128)} %sea_hbm.1) | copy-start | bytes 196612
  0.0 22.9 %copy-start.4 = (s32[64]{0:T(128)S(1)}, s32[64]{0:T(128)}, u32[]{:S(2)}) copy-start(s32[64]{0:T(128)} %partner.1) | copy-start | bytes 772
  1.7 21.2 %all-to-all-start = ((f32[128,2,128]{2,1,0:T(2,128)}), f32[128,2,128]{2,1,0:T(2,128)S(1)}, u32[]{:S(2)}, u32[]{:S(2)}) async-start(f32[128,2,128]{2,1,0:T(2,128)} %bitcast.18), calls=%async_computation | async-start | bytes 262144 | tf_op jit(solution)/shard_map/all_to_all | solution.py:427
  15.4 13.5 %collective-permute-start = (f32[2,136,256]{2,1,0:T(8,128)}, f32[2,136,256]{2,1,0:T(8,128)}, u32[]{:S(2)}, u32[]{:S(2)}) collective-permute-start(f32[2,136,256]{2,1,0:T(8,128)} %get-tuple-element.12.sent_near), channel_id=1, source_target_pairs={{0,1},{1,0},{2,3},{3,2},{4,5},{5,4},{6,7},{7,6},{8,9},{9,8},{10,11... | collective-permute-start | bytes 835592 | tf_op jit(solution)/shard_map/ppermute | solution.py:433
  15.5 13.4 %collective-permute-start.1 = (f32[2,136,256]{2,1,0:T(8,128)}, f32[2,136,256]{2,1,0:T(8,128)}, u32[]{:S(2)}, u32[]{:S(2)}) collective-permute-start(f32[2,136,256]{2,1,0:T(8,128)} %get-tuple-element.13.sent_far), channel_id=1, source_target_pairs={{0,63},{1,2},{2,1},{3,4},{4,3},{5,6},{6,5},{7,8},{8,7},{9,10},{10,... | collective-permute-start | bytes 835592 | tf_op jit(solution)/shard_map/ppermute | solution.py:434
  22.9 6.0 %copy-start.1 = (f32[64,256]{1,0:T(8,128)S(1)}, f32[64,256]{1,0:T(8,128)}, u32[]{:S(2)}) copy-start(f32[64,256]{1,0:T(8,128)} %get-tuple-element.14.mask) | copy-start | bytes 196612
  22.9 6.0 %copy-start.2 = (f32[1,2,64]{2,1,0:T(2,128)S(1)}, f32[1,2,64]{2,1,0:T(2,128)}, u32[]{:S(2)}) copy-start(f32[1,2,64]{2,1,0:T(2,128)} %param.7) | copy-start | bytes 1540
  22.9 6.0 %copy-start.3 = (f32[1,2]{1,0:T(1,128)S(1)}, f32[1,2]{1,0:T(1,128)}, u32[]{:S(2)}) copy-start(f32[1,2]{1,0:T(1,128)} %param.8) | copy-start | bytes 28
  24.3 22.5 %all-to-all-start.1 = ((f32[128,2,128]{2,1,0:T(2,128)}), f32[128,2,128]{2,1,0:T(2,128)S(1)}, u32[]{:S(2)}, u32[]{:S(2)}) async-start(f32[128,2,128]{2,1,0:T(2,128)} %bitcast.8), calls=%async_computation.1 | async-start | bytes 262144 | tf_op jit(solution)/shard_map/all_to_all | solution.py:430

commit v3 on v2

--- a/solution.py
+++ b/solution.py
@@ -9,7 +9,7 @@
 
 BOTH = ("comp", "tile")
 CHUNK = 8
-UNROLL = 8
+BLOCK = 16
 MIB = 1 << 20
 
 
@@ -31,7 +31,7 @@
 
 def mix_kernel(
     place, hz_any, vt_any, state, sent_near, sent_far, got_near, got_far, mask, out, base, aux,
-    mine, halo, strip_sem, hz, vt, hcol, raw, s1, res, edge, split, wet, rate_sem, in_sem, out_sem,
+    mine, halo, strip_sem, hz, vt, hcol, raw, s0, s1, res, edge, split, wet, rate_sem, in_sem, out_sem,
 ):
     fields, levels, rows, width = state.shape
     per = levels // CHUNK
@@ -54,11 +54,6 @@
             pltpu.make_async_copy(res.at[(k, *where)], out.at[(*where, slice(None), lanes)], out_sem.at[q, k])
             for k, lanes in enumerate(sides)
         ]
-
-    @pl.loop(0, total)
-    def _(q):
-        for copy in load(q):
-            copy.start()
 
     odd = place[0] % 2
     strips = [
@@ -73,6 +68,12 @@
     rates = [pltpu.make_async_copy(hz_any, hz, rate_sem.at[0]), pltpu.make_async_copy(vt_any, vt, rate_sem.at[1])]
     for copy in rates:
         copy.start()
+
+    @pl.loop(0, total)
+    def _(q):
+        for copy in load(q):
+            copy.start()
+
     for copy in rates:
         copy.wait()
 
@@ -120,53 +121,69 @@
         for r in range(nrow):
             wet[pl.ds(8 * r, 8), lanes] = split[k, pl.ds(r, 8, stride=nrow), :]
 
-    def substep(get, src, f, l, ahead, behind):
+    def pack(f, l):
+        for r in range(nrow):
+            s0[f, l, pl.ds(8 * r, 8), :] = spread(raw, f, l, r)
+
+    def substep(src, f, base, i, ahead, behind):
+        l = base + i
         h, v = hz[f, l], vt[f]
         c0 = 1.0 - 4.0 * h - 2.0 * v
-        lo, hi = jnp.maximum(l - 1, 0), jnp.minimum(l + 1, levels - 1)
+        lo = l - 1 if i else jnp.maximum(l - 1, 0)
+        hi = l + 1 if i < BLOCK - 1 else jnp.minimum(l + 1, levels - 1)
         p = f * levels + l
-        x = [get(src, f, l, r) for r in range(nrow)]
+        x = [src[f, l, pl.ds(8 * r, 8), :] for r in range(nrow)]
         above = jnp.where(top, jnp.broadcast_to(ahead[pl.ds(p, 1), :], (8, width)), pltpu.roll(x[-1], 1, 0))
         under = jnp.where(bottom, jnp.broadcast_to(behind[pl.ds(p, 1), :], (8, width)), pltpu.roll(x[0], 7, 0))
         for r in range(nrow):
+            at = pl.ds(8 * r, 8)
             near = (x[r - 1] if r else above) + (x[r + 1] if r < nrow - 1 else under)
-            vert = get(src, f, lo, r) + get(src, f, hi, r)
+            vert = src[f, lo, at, :] + src[f, hi, at, :]
             new = x[r] * c0 + h * (near + beside(x[r])) + v * vert
-            yield r, new * wet[pl.ds(8 * r, 8), :]
-
-    def first(f, l):
-        for r, new in substep(spread, raw, f, l, before.at[1], after.at[0]):
-            s1[f, l, pl.ds(8 * r, 8), :] = new
-
-    def second(f, l):
-        for r, new in substep(packed, s1, f, l, edge.at[0], edge.at[1]):
-            for k, lanes in enumerate(sides):
-                res[k, f, l, pl.ds(r, 8, stride=nrow), :] = new[:, k * half : (k + 1) * half]
+            yield r, new * wet[at, :]
+
+    def first(f, base, i):
+        pack(f, base + i + 1 if i < BLOCK - 1 else jnp.minimum(base + i + 1, levels - 1))
+        for r, new in substep(s0, f, base, i, before.at[1], after.at[0]):
+            s1[f, base + i, pl.ds(8 * r, 8), :] = new
+
+    def second(f, base, i):
+        for r, new in substep(s1, f, base, i, edge.at[0], edge.at[1]):
+            for k in range(2):
+                res[k, f, base + i, pl.ds(r, 8, stride=nrow), :] = new[:, k * half : (k + 1) * half]
+
+    blocks, step = fields * levels // BLOCK, BLOCK // CHUNK
 
     for copy in load(0):
         copy.wait()
 
-    @pl.loop(0, total + 1)
+    @pl.loop(0, blocks + 1)
     def _(q):
-        @pl.when(q < total - 1)
+        for j in range(1, step + 1):
+            @pl.when(q * step + j < total)
+            def _(j=j):
+                for copy in load(q * step + j):
+                    copy.wait()
+
+        @pl.when(q * BLOCK % levels == 0)
         def _():
-            for copy in load(q + 1):
-                copy.wait()
-
-        @pl.when(q < total)
+            pack(jnp.minimum(q * BLOCK // levels, fields - 1), 0)
+
+        @pl.when(q < blocks)
         def _():
-            @pl.loop(0, CHUNK, unroll=UNROLL)
-            def _(i):
-                first(q // per, (q % per) * CHUNK + i)
+            f, l = q * BLOCK // levels, q * BLOCK % levels
+            for i in range(BLOCK):
+                first(f, l, i)
 
         @pl.when(q > 0)
         def _():
-            @pl.loop(0, CHUNK, unroll=UNROLL)
-            def _(i):
-                second((q - 1) // per, ((q - 1) % per) * CHUNK + i)
-
-            for copy in store(q - 1):
-                copy.start()
+            f, l = (q - 1) * BLOCK // levels, (q - 1) * BLOCK % levels
+            for i in range(BLOCK):
+                second(f, l, i)
+
+            for j in range(step):
+                for copy in store((q - 1) * step + j):
+                    copy.start()
 
         @pl.when(q == 1)
         def _():
@@ -184,7 +201,6 @@
     planes = nf * levels
     vmem = pl.BlockSpec(memory_space=pltpu.VMEM)
     smem = pl.BlockSpec(memory_space=pltpu.SMEM)
-    anyw = pl.BlockSpec(memory_space=pl.ANY)
     hbm = pl.BlockSpec(memory_space=pltpu.HBM)
     total = nf * levels // CHUNK
     halved = (2, nf, levels, rows, width // 2)
@@ -195,7 +211,7 @@
             jax.ShapeDtypeStruct((3, rows, width), jnp.float32),
             jax.ShapeDtypeStruct((8, width), jnp.float32),
         ),
-        in_specs=[smem, hbm, hbm, hbm, anyw, anyw, anyw, anyw, vmem],
+        in_specs=[smem, hbm, hbm, hbm, vmem, vmem, vmem, vmem, vmem],
         out_specs=(hbm, vmem, vmem),
         scratch_shapes=[
             pltpu.VMEM((2, 2, planes + 8, width), jnp.float32),
@@ -205,6 +221,7 @@
             pltpu.SMEM((nf,), jnp.float32),
             pltpu.VMEM((planes, width // 2), jnp.float32),
             pltpu.VMEM(halved, jnp.float32),
+            pltpu.VMEM(fields.shape, jnp.float32),
             pltpu.VMEM(fields.shape, jnp.float32),
             pltpu.VMEM(halved, jnp.float32),
             pltpu.VMEM((2, planes, width), jnp.float32),

time: 48.2 us -> 45.1 us (0.936)
  Pallas kernels: 24.3 us -> 21.2 us
    pallas_call x1, Pallas kernels: 17.8 us -> 14.7 us  [mix(): pl.pallas_call(mix_kernel, out_shape=(jax.ShapeDtypeStruct(fields.shape,...]
  transfers between devices with their start and end apart: 4 -> 4, of which waited for: 0 -> 0; matrix products, arithmetic and copies ran while one was open for 0% -> 0% of each run, Pallas kernels for 45% -> 42%
where the time goes in v3:
time: 45.1 us; the launch traced here: 44.6 us
  starting transfers between devices  23.3 us (52%)
  Pallas kernels  21.2 us (47%)
    pallas_call x1, Pallas kernels, mix(): pl.pallas_call(mix_kernel, out_shape=(jax.ShapeDtypeStruct(fields.shape,...  14.7 us
    all_to_all x1, starting transfers between devices, per_device(): got = lax.all_to_all(outgoing, BOTH, 0, 0, tiled=True)  11.1 us
    ppermute x1, starting transfers between devices, per_device(): lax.ppermute(sent_far, 'tile', [(i, (i + 2 * (i % 2) - 1) % ntile) for i...  7.43 us
    all_to_all x1, starting transfers between devices, per_device(): back = lax.all_to_all(pieces, BOTH, 0, 0, tiled=True)  4.6 us
    pallas_call x1, Pallas kernels, edges(): pl.pallas_call(edge_kernel, out_shape=(shape, shape), in_specs=[smem, sme...  2.55 us
    pallas_call x1, Pallas kernels, prep(): pl.pallas_call(prep_kernel, out_shape=(jax.ShapeDtypeStruct((4 * rows, wi...  1.65 us
    pallas_call x1, Pallas kernels, flux_pieces(): pl.pallas_call(flux_kernel, out_shape=jax.ShapeDtypeStruct(got.shape, jnp...  1.32 us
    pallas_call x1, Pallas kernels, add_flux(): pl.pallas_call(add_kernel, out_shape=jax.ShapeDtypeStruct(whole.shape, jn...  0.95 us
  transfers between devices with their start and end apart: 4, of which 0 were waited for; matrix products, arithmetic and copies ran while one was open for 0% of the time, Pallas kernels for 42%

profile of v3, /device:TPU:0, one launch (start us, length us, event | category | flops | bytes accessed | tf_op | source)
XLA Modules:
  0.0 44.6 jit_solution(4159350715373040625)
XLA Ops:
  0.0 0.0 copy-start
  0.0 0.0 copy-start.4
  0.0 1.6 %prep.1 = (f32[256,128]{1,0:T(8,128)}, f32[64,256]{1,0:T(8,128)}) custom-call(s32[1]{0:T(128)} %bitcast.5.atmos, f32[2,64,64,256]{3,2,1,0:T(8,128)} %bitcast.15, f32[64,256]{1,0:T(8,128)} %coef_hbm.1, s32[64,256]{1,0:T(8,128)} %sea_hbm.1), custom_call_target="tpu_custom_call" | custom-call | flops 49152 | bytes 393216 | tf_op jit(solution)/shard_map/prep/pallas_call | solution.py:267
  1.7 11.1 %all-to-all-start = ((f32[128,2,128]{2,1,0:T(2,128)}), f32[128,2,128]{2,1,0:T(2,128)S(1)}, u32[]{:S(2)}, u32[]{:S(2)}) async-start(f32[128,2,128]{2,1,0:T(2,128)} %bitcast.18), calls=%async_computation | async-start | bytes 262144 | tf_op jit(solution)/shard_map/all_to_all | solution.py:444
  12.8 0.0 copy-done
  12.8 2.5 %edges.1 = (f32[2,136,256]{2,1,0:T(8,128)}, f32[2,136,256]{2,1,0:T(8,128)}) custom-call(s32[1]{0:T(128)} %bitcast.1.place, s32[1]{0:T(128)} %bitcast.5.atmos, f32[2,64,64,256]{3,2,1,0:T(8,128)} %bitcast.16, s32[64,256]{1,0:T(8,128)S(1)} %copy-done), custom_call_target="tpu_custom_call" | custom-call | bytes 4194304 | tf_op jit(solution)/shard_map/edges/pallas_call | solution.py:329
  15.4 0.1 collective-permute-start
  15.5 7.4 %collective-permute-start.1 = (f32[2,136,256]{2,1,0:T(8,128)}, f32[2,136,256]{2,1,0:T(8,128)}, u32[]{:S(2)}, u32[]{:S(2)}) collective-permute-start(f32[2,136,256]{2,1,0:T(8,128)} %get-tuple-element.13.sent_far), channel_id=1, source_target_pairs={{0,63},{1,2},{2,1},{3,4},{4,3},{5,6},{6,5},{7,8},{8,7},{9,10},{10,... | collective-permute-start | bytes 835592 | tf_op jit(solution)/shard_map/ppermute | solution.py:451
  22.9 0.0 all-to-all-done
  22.9 0.0 copy-done.4
  22.9 0.0 copy-start.1
  22.9 0.0 copy-start.2
  22.9 0.0 copy-start.3
  22.9 1.3 %flux.1 = f32[256,128]{1,0:T(8,128)} custom-call(s32[64]{0:T(128)S(1)} %copy-done.4, s32[1]{0:T(128)} %bitcast.1.place, f32[256,128]{1,0:T(8,128)S(1)} %bitcast.12), custom_call_target="tpu_custom_call" | custom-call | flops 999999995904 | bytes 262144 | tf_op jit(solution)/shard_map/flux/pallas_call | solution.py:366
  24.3 4.6 %all-to-all-start.1 = ((f32[128,2,128]{2,1,0:T(2,128)}), f32[128,2,128]{2,1,0:T(2,128)S(1)}, u32[]{:S(2)}, u32[]{:S(2)}) async-start(f32[128,2,128]{2,1,0:T(2,128)} %bitcast.8), calls=%async_computation.1 | async-start | bytes 262144 | tf_op jit(solution)/shard_map/all_to_all | solution.py:447
  28.9 0.0 collective-permute-done.got_near
  28.9 0.0 collective-permute-done.1.got_far
  28.9 0.0 copy-done.1
  28.9 0.0 copy-done.2
  28.9 0.0 copy-done.3
  28.9 14.7 %mix.1 = (f32[2,64,64,256]{3,2,1,0:T(8,128)}, f32[3,64,256]{2,1,0:T(8,128)S(1)}, f32[8,256]{1,0:T(8,128)S(1)}) custom-call(s32[1]{0:T(128)} %bitcast.1.place, f32[2,64]{1,0:T(2,128)S(1)} %bitcast.13, f32[2]{0:T(128)S(1)} %bitcast.14, f32[2,64,64,256]{3,2,1,0:T(8,128)} %bitcast.17, f32[2,136,256]{2,1,0:T(8,128)} %get-tuple-element.12.sent_near, ...), custom_call_target="tpu_custom_call" | custom-call | flops 54525952 | bytes 16777216 | tf_op jit(solution)/shard_map/mix/pallas_call | solution.py:207
  43.7 0.0 all-to-all-done.1
  43.7 1.0 %add.1 = f32[2,64,64,256]{3,2,1,0:T(8,128)} custom-call(f32[1]{0:T(128)} %bitcast.sign, f32[3,64,256]{2,1,0:T(8,128)S(1)} %get-tuple-element.15.base, f32[256,128]{1,0:T(8,128)S(1)} %bitcast.11, f32[64,256]{1,0:T(8,128)S(1)} %copy-done.1, f32[8,256]{1,0:T(8,128)S(1)} %get-tuple-element.17.aux, ...), custom_call_target="tpu_custom_call", output_to_operand_aliasing={{}: (5, {})} | custom-call | flops 491520 | bytes 524288 | tf_op jit(solution)/shard_map/add/pallas_call | solution.py:425
Async XLA Ops:
  0.0 12.8 %copy-start = (s32[64,256]{1,0:T(8,128)S(1)}, s32[64,256]{1,0:T(8,128)}, u32[]{:S(2)}) copy-start(s32[64,256]{1,0:T(8,128)} %sea_hbm.1) | copy-start | bytes 196612
  0.0 22.9 %copy-start.4 = (s32[64]{0:T(128)S(1)}, s32[64]{0:T(128)}, u32[]{:S(2)}) copy-start(s32[64]{0:T(128)} %partner.1) | copy-start | bytes 772
  1.7 21.2 %all-to-all-start = ((f32[128,2,128]{2,1,0:T(2,128)}), f32[128,2,128]{2,1,0:T(2,128)S(1)}, u32[]{:S(2)}, u32[]{:S(2)}) async-start(f32[128,2,128]{2,1,0:T(2,128)} %bitcast.18), calls=%async_computation | async-start | bytes 262144 | tf_op jit(solution)/shard_map/all_to_all | solution.py:444
  15.4 13.5 %collective-permute-start = (f32[2,136,256]{2,1,0:T(8,128)}, f32[2,136,256]{2,1,0:T(8,128)}, u32[]{:S(2)}, u32[]{:S(2)}) collective-permute-start(f32[2,136,256]{2,1,0:T(8,128)} %get-tuple-element.12.sent_near), channel_id=1, source_target_pairs={{0,1},{1,0},{2,3},{3,2},{4,5},{5,4},{6,7},{7,6},{8,9},{9,8},{10,11... | collective-permute-start | bytes 835592 | tf_op jit(solution)/shard_map/ppermute | solution.py:450
  15.5 13.4 %collective-permute-start.1 = (f32[2,136,256]{2,1,0:T(8,128)}, f32[2,136,256]{2,1,0:T(8,128)}, u32[]{:S(2)}, u32[]{:S(2)}) collective-permute-start(f32[2,136,256]{2,1,0:T(8,128)} %get-tuple-element.13.sent_far), channel_id=1, source_target_pairs={{0,63},{1,2},{2,1},{3,4},{4,3},{5,6},{6,5},{7,8},{8,7},{9,10},{10,... | collective-permute-start | bytes 835592 | tf_op jit(solution)/shard_map/ppermute | solution.py:451
  22.9 6.0 %copy-start.1 = (f32[64,256]{1,0:T(8,128)S(1)}, f32[64,256]{1,0:T(8,128)}, u32[]{:S(2)}) copy-start(f32[64,256]{1,0:T(8,128)} %get-tuple-element.14.mask) | copy-start | bytes 196612
  22.9 6.0 %copy-start.2 = (f32[1,2,64]{2,1,0:T(2,128)S(1)}, f32[1,2,64]{2,1,0:T(2,128)}, u32[]{:S(2)}) copy-start(f32[1,2,64]{2,1,0:T(2,128)} %param.7) | copy-start | bytes 1540
  22.9 6.0 %copy-start.3 = (f32[1,2]{1,0:T(1,128)S(1)}, f32[1,2]{1,0:T(1,128)}, u32[]{:S(2)}) copy-start(f32[1,2]{1,0:T(1,128)} %param.8) | copy-start | bytes 28
  24.3 19.4 %all-to-all-start.1 = ((f32[128,2,128]{2,1,0:T(2,128)}), f32[128,2,128]{2,1,0:T(2,128)S(1)}, u32[]{:S(2)}, u32[]{:S(2)}) async-start(f32[128,2,128]{2,1,0:T(2,128)} %bitcast.8), calls=%async_computation.1 | async-start | bytes 262144 | tf_op jit(solution)/shard_map/all_to_all | solution.py:447

commit v4 on v3

v4 whole, which is shorter than its diff:
```python
import functools

import jax
import jax.numpy as jnp
from jax import lax
from jax.experimental import pallas as pl
from jax.experimental.pallas import tpu as pltpu
from jax.sharding import PartitionSpec as P

BOTH = ("comp", "tile")
CHUNK = 8
BLOCK = 16
MIB = 1 << 20


def row_ids(rows, width):
    return lax.broadcasted_iota(jnp.int32, (rows, width), 0)


def beside(x):
    half = x.shape[-1] // 2
    a, b = x[:, :half], x[:, half:]
    lane = lax.broadcasted_iota(jnp.int32, a.shape, 1)
    first, last = lane == 0, lane == half - 1
    ra, rb = pltpu.roll(a, 1, 1), pltpu.roll(b, 1, 1)
    la, lb = pltpu.roll(a, half - 1, 1), pltpu.roll(b, half - 1, 1)
    left = jnp.where(first, rb, ra) + jnp.where(last, lb, la)
    right = jnp.where(first, ra, rb) + jnp.where(last, la, lb)
    return jnp.concatenate([left, right], 1)


def mix_kernel(
    hz_any, vt_any, state, sent_near, sent_far, got_near, got_far, mask, out, base, aux,
    mine, halo, strip_sem, hz, vt, hcol, raw, s0, s1, res, edge, split, wet, rate_sem, in_sem, out_sem,
):
    planes, rows, width = state.shape
    fields, levels = hz.shape
    total = planes // CHUNK
    half = width // 2
    sides = [pl.ds(k * half, half) for k in range(2)]

    def load(q):
        at = pl.ds(q * CHUNK, CHUNK)
        return [
            pltpu.make_async_copy(state.at[at, :, lanes], raw.at[k, at], in_sem.at[q, k])
            for k, lanes in enumerate(sides)
        ]

    def store(q):
        at = pl.ds(q * CHUNK, CHUNK)
        return [
            pltpu.make_async_copy(res.at[k, at], out.at[at, :, lanes], out_sem.at[q, k])
            for k, lanes in enumerate(sides)
        ]

    odd = lax.axis_index("tile") % 2
    strips = [
        pltpu.make_async_copy(src, dst.at[slot], strip_sem.at[i])
        for i, (src, dst, slot) in enumerate(
            ((sent_near, mine, 1 - odd), (sent_far, mine, odd), (got_near, halo, 1 - odd), (got_far, halo, odd))
        )
    ]
    for copy in strips:
        copy.start()
    rates = [pltpu.make_async_copy(hz_any, hz, rate_sem.at[0]), pltpu.make_async_copy(vt_any, vt, rate_sem.at[1])]
    for copy in rates:
        copy.start()

    @pl.loop(0, total)
    def _(q):
        for copy in load(q):
            copy.start()

    for copy in rates:
        copy.wait()

    for p in range(planes):
        hcol[p : p + 1, :] = jnp.full((1, half), hz[p // levels, p % levels], jnp.float32)

    for copy in strips:
        copy.wait()
    mine_first, mine_last, before, after = mine.at[0], mine.at[1], halo.at[0], halo.at[1]
    for j in range(4):
        aux[j : j + 1, :] = jnp.full((1, width), (hz[0, 0], hz[0, 1], vt[0], vt[0])[j], jnp.float32)
    aux[4:5, :] = before[1, planes : planes + 1, :]
    aux[5:6, :] = after[0, planes : planes + 1, :]

    level = row_ids(levels, width)
    for side, (x2, x1, x0, m) in enumerate(
        (
            (before.at[0], before.at[1], mine_first.at[0], before[1, planes : planes + 1, :]),
            (after.at[1], after.at[0], mine_last.at[1], after[0, planes : planes + 1, :]),
        )
    ):
        for f in range(fields):
            at = pl.ds(f * levels, levels)
            x = x1[at, :]
            lap = x2[at, :] + x0[at, :] + beside(x)
            below = jnp.where(level == 0, x, pltpu.roll(x, 1, 0))
            above = jnp.where(level == levels - 1, x, pltpu.roll(x, levels - 1, 0))
            h = jnp.concatenate([hcol[at, :]] * 2, 1)
            v = vt[f]
            new = x * (1.0 - 4.0 * h - 2.0 * v) + h * lap + v * (above + below)
            edge[side, at, :] = new * m

    row = row_ids(8, width)
    top, bottom = row == 0, row == 7
    nrow = rows // 8

    for k, lanes in enumerate(sides):
        split[k] = mask[:, lanes]
        for r in range(nrow):
            wet[pl.ds(8 * r, 8), lanes] = split[k, pl.ds(r, 8, stride=nrow), :]

    def pack(p):
        for r in range(nrow):
            s0[p, pl.ds(8 * r, 8), :] = jnp.concatenate([raw[k, p, pl.ds(r, 8, stride=nrow), :] for k in range(2)], 1)

    def substep(src, p, lo, hi, ahead, behind):
        f = p // levels
        h, v = hz[f, p % levels], vt[f]
        c0 = 1.0 - 4.0 * h - 2.0 * v
        x = [src[p, pl.ds(8 * r, 8), :] for r in range(nrow)]
        above = jnp.where(top, jnp.broadcast_to(ahead[pl.ds(p, 1), :], (8, width)), pltpu.roll(x[-1], 1, 0))
        under = jnp.where(bottom, jnp.broadcast_to(behind[pl.ds(p, 1), :], (8, width)), pltpu.roll(x[0], 7, 0))
        for r in range(nrow):
            at = pl.ds(8 * r, 8)
            near = (x[r - 1] if r else above) + (x[r + 1] if r < nrow - 1 else under)
            vert = src[lo, at, :] + src[hi, at, :]
            new = x[r] * c0 + h * (near + beside(x[r])) + v * vert
            yield r, new * wet[at, :]

    def first(start, i):
        p = start + i
        pack(p + 1 if i < BLOCK - 1 else jnp.minimum(p + 1, planes - 1))
        lo = p - 1 if i else jnp.where(p % levels == 0, p, p - 1)
        hi = p + 1 if i < BLOCK - 1 else jnp.where(p % levels == levels - 1, p, p + 1)
        for r, new in substep(s0, p, lo, hi, before.at[1], after.at[0]):
            s1[p, pl.ds(8 * r, 8), :] = new

    def second_at(p, lo, hi):
        for r, new in substep(s1, p, lo, hi, edge.at[0], edge.at[1]):
            for k in range(2):
                res[k, p, pl.ds(r, 8, stride=nrow), :] = new[:, k * half : (k + 1) * half]

    def second(start, i):
        p = start + i - 1 if i else jnp.maximum(start - 1, 0)
        lo = p - 1 if i > 1 else jnp.where(p % levels == 0, p, p - 1)
        hi = p + 1 if i else jnp.where(p % levels == levels - 1, p, p + 1)
        second_at(p, lo, hi)

    blocks, step = planes // BLOCK, BLOCK // CHUNK

    def arrive(q):
        for copy in load(q):
            copy.wait()

    def leave(q):
        for copy in store(q):
            copy.start()

    for j in range(step + 1):
        arrive(j)
    pack(0)
    for i in range(BLOCK):
        first(0, i)

    @pl.loop(1, blocks)
    def _(q):
        for j in range(1, step + 1):
            @pl.when(q * step + j < total)
            def _(j=j):
                arrive(q * step + j)

        now = q * BLOCK
        for i in range(BLOCK):
            second(now - BLOCK, i)
        for i in range(BLOCK):
            first(now, i)

        @pl.when(q > 1)
        def _():
            leave((q - 1) * step - 1)

        for j in range(step - 1):
            leave((q - 1) * step + j)

        @pl.when(q == 1)
        def _():
            for k, lanes in enumerate(sides):
                base[:, :, lanes] = res[k, 0:3]

    for i in range(BLOCK):
        second(planes - BLOCK, i)
        if i % CHUNK == 0:
            leave(total - step - 1 + i // CHUNK)
    second_at(planes - 1, planes - 2, planes - 1)
    leave(total - 1)

    @pl.loop(0, total)
    def _(q):
        for copy in store(q):
            copy.wait()


def mix(fields, hz, vt, sent_near, sent_far, got_near, got_far, mask):
    nf, levels, rows, width = fields.shape
    planes = nf * levels
    flat = (planes, rows, width)
    vmem = pl.BlockSpec(memory_space=pltpu.VMEM)
    hbm = pl.BlockSpec(memory_space=pltpu.HBM)
    total = nf * levels // CHUNK
    halved = (2, planes, rows, width // 2)
    whole, base, aux = pl.pallas_call(
        mix_kernel,
        out_shape=(
            jax.ShapeDtypeStruct(flat, jnp.float32),
            jax.ShapeDtypeStruct((3, rows, width), jnp.float32),
            jax.ShapeDtypeStruct((8, width), jnp.float32),
        ),
        in_specs=[hbm, hbm, hbm, vmem, vmem, vmem, vmem, vmem],
        out_specs=(hbm, vmem, vmem),
        scratch_shapes=[
            pltpu.VMEM((2, 2, planes + 8, width), jnp.float32),
            pltpu.VMEM((2, 2, planes + 8, width), jnp.float32),
            pltpu.SemaphoreType.DMA((4,)),
            pltpu.SMEM((nf, levels), jnp.float32),
            pltpu.SMEM((nf,), jnp.float32),
            pltpu.VMEM((planes, width // 2), jnp.float32),
            pltpu.VMEM(halved, jnp.float32),
            pltpu.VMEM(flat, jnp.float32),
            pltpu.VMEM(flat, jnp.float32),
            pltpu.VMEM(halved, jnp.float32),
            pltpu.VMEM((2, planes, width), jnp.float32),
            pltpu.VMEM((2, rows, width // 2), jnp.float32),
            pltpu.VMEM((rows, width), jnp.float32),
            pltpu.SemaphoreType.DMA((2,)),
            pltpu.SemaphoreType.DMA((total, 2)),
            pltpu.SemaphoreType.DMA((total, 2)),
        ],
        compiler_params=pltpu.CompilerParams(vmem_limit_bytes=46 * MIB),
        cost_estimate=pl.CostEstimate(flops=26 * fields.size, bytes_accessed=8 * fields.size, transcendentals=0),
        name="mix",
    )(hz, vt, fields.reshape(flat), sent_near, sent_far, got_near, got_far, mask)
    return whole.reshape(fields.shape), base, aux


def prep_kernel(state, coef_hbm, sea_hbm, out, wet, surface, coef, sea, sem):
    rows, width = coef.shape
    half = width // 2
    copies = [
        pltpu.make_async_copy(state.at[0, 0], surface, sem.at[0]),
        pltpu.make_async_copy(coef_hbm, coef, sem.at[1]),
        pltpu.make_async_copy(sea_hbm, sea, sem.at[2]),
    ]
    for copy in copies:
        copy.start()
    for copy in copies:
        copy.wait()
    ocean = sea[...].astype(jnp.float32)
    mine = lax.axis_index("comp") == 0
    second = jnp.where(mine, coef[...], ocean)
    wet[...] = jnp.where(mine, jnp.ones_like(ocean), ocean)
    for k in range(2):
        lanes = slice(k * half, (k + 1) * half)
        out[pl.ds(2 * k * rows, rows, stride=2), :] = surface[:, lanes]
        out[pl.ds(2 * k * rows + 1, rows, stride=2), :] = second[:, lanes]


def prep(fields, coef, sea):
    vmem = pl.BlockSpec(memory_space=pltpu.VMEM)
    hbm = pl.BlockSpec(memory_space=pltpu.HBM)
    rows, width = coef.shape
    return pl.pallas_call(
        prep_kernel,
        out_shape=(
            jax.ShapeDtypeStruct((4 * rows, width // 2), jnp.float32),
            jax.ShapeDtypeStruct((rows, width), jnp.float32),
        ),
        in_specs=[hbm, hbm, hbm],
        out_specs=(vmem, vmem),
        scratch_shapes=[
            pltpu.VMEM((rows, width), jnp.float32),
            pltpu.VMEM((rows, width), jnp.float32),
            pltpu.VMEM((rows, width), jnp.int32),
            pltpu.SemaphoreType.DMA((3,)),
        ],
        compiler_params=pltpu.CompilerParams(vmem_limit_bytes=60 * MIB),
        cost_estimate=pl.CostEstimate(flops=3 * coef.size, bytes_accessed=24 * coef.size, transcendentals=0),
        name="prep",
    )(fields, coef, sea)


def edge_kernel(state, sea_any, near, far, stage, sea, sem):
    nf, levels, rows, width = state.shape
    planes = nf * levels
    copies = [
        pltpu.make_async_copy(state.at[f, :, pl.ds(at, 8), :], stage.at[side, f], sem.at[side, f])
        for side, at in enumerate((0, rows - 8))
        for f in range(nf)
    ]
    mask_copy = pltpu.make_async_copy(sea_any, sea, sem.at[2, 0])
    mask_copy.start()
    for copy in copies:
        copy.start()
    mask_copy.wait()

    def fill(first, last):
        for side, (out, at) in enumerate(((first, 0), (last, 6))):
            for f in range(nf):
                copies[side * nf + f].wait()
                for j in range(2):
                    for g in range(0, levels, 8):
                        p = f * levels + g
                        out[j, p : p + 8, :] = stage[side, f, g : g + 8, at + j, :]
            for j in range(2):
                row = side * (rows - 2) + j
                wet = jnp.where(lax.axis_index("comp") == 0, 1.0, sea[row : row + 1, :].astype(jnp.float32))
                out[j, planes : planes + 8, :] = jnp.broadcast_to(wet, (8, width))

    even = lax.axis_index("tile") % 2 == 0

    @pl.when(even)
    def _():
        fill(far, near)

    @pl.when(jnp.logical_not(even))
    def _():
        fill(near, far)


def edges(fields, sea):
    vmem = pl.BlockSpec(memory_space=pltpu.VMEM)
    anyw = pl.BlockSpec(memory_space=pl.ANY)
    hbm = pl.BlockSpec(memory_space=pltpu.HBM)
    nf, levels, _, width = fields.shape
    shape = jax.ShapeDtypeStruct((2, nf * levels + 8, width), jnp.float32)
    return pl.pallas_call(
        edge_kernel,
        out_shape=(shape, shape),
        in_specs=[hbm, anyw],
        out_specs=(vmem, vmem),
        scratch_shapes=[
            pltpu.VMEM((2, nf, levels, 8, width), jnp.float32),
            pltpu.VMEM(sea.shape, jnp.int32),
            pltpu.SemaphoreType.DMA((3, nf)),
        ],
        compiler_params=pltpu.CompilerParams(vmem_limit_bytes=46 * MIB),
        cost_estimate=pl.CostEstimate(flops=0, bytes_accessed=4 * MIB, transcendentals=0),
        name="edges",
    )(fields, sea)


def flux_kernel(partner, got, back, theirs, mine, other):
    tiles = got.shape[0] // 4
    for t in range(tiles):
        theirs[2 * t : 2 * t + 2, :] = got[pl.ds(2 * tiles + 2 * partner[t], 2), :]
    odd, even = pl.ds(1, tiles, stride=2), pl.ds(0, tiles, stride=2)
    flux = got[odd, :] * (got[even, :] - theirs[even, :]) * theirs[odd, :]
    mine[...] = flux
    for t in range(tiles):
        other[pl.ds(partner[t], 1), :] = mine[t : t + 1, :]
    turned = other[...]
    shift = jnp.where(lax.axis_index("tile") < 2, tiles - 1, 1)
    back[even, :] = flux
    back[odd, :] = pltpu.roll(flux, shift, 0)
    back[pl.ds(2 * tiles, tiles, stride=2), :] = turned
    back[pl.ds(2 * tiles + 1, tiles, stride=2), :] = pltpu.roll(turned, shift, 0)


def flux_pieces(partner, got):
    vmem = pl.BlockSpec(memory_space=pltpu.VMEM)
    smem = pl.BlockSpec(memory_space=pltpu.SMEM)
    tiles, half = got.shape[0] // 4, got.shape[1]
    return pl.pallas_call(
        flux_kernel,
        out_shape=jax.ShapeDtypeStruct(got.shape, jnp.float32),
        in_specs=[smem, vmem],
        out_specs=vmem,
        scratch_shapes=[
            pltpu.VMEM((2 * tiles, half), jnp.float32),
            pltpu.VMEM((tiles, half), jnp.float32),
            pltpu.VMEM((tiles, half), jnp.float32),
        ],
        compiler_params=pltpu.CompilerParams(vmem_limit_bytes=2 * MIB),
        cost_estimate=pl.CostEstimate(flops=3 * 10**10, bytes_accessed=8 * got.size, transcendentals=0),
        name="flux",
    )(partner, got)


def add_kernel(base, back, mask, aux, whole, out, ext, three, sem):
    del whole
    rows, width = mask.shape
    half = width // 2
    s = jnp.where(lax.axis_index("comp") == 0, -1.0, 1.0).astype(jnp.float32)
    h0, h1, v = (aux[j : j + 1, :] for j in range(3))
    zero_pad = jnp.zeros((8, width), jnp.float32)
    ext[0:8, :] = zero_pad
    ext[8 + rows : 16 + rows, :] = zero_pad
    for k in range(2):
        lanes = pl.ds(k * half, half)
        at = 2 * k * rows
        ext[8 : 8 + rows, lanes] = back[pl.ds(at, rows, stride=2), :] * s
        for j in range(2):
            ext[6 + j : 7 + j, lanes] = back[pl.ds(at + 2 * (rows - 2 + j) + 1, 1), :] * s
            ext[8 + rows + j : 9 + rows + j, lanes] = back[pl.ds(at + 2 * j + 1, 1), :] * s

    total = rows + 16
    m = jnp.concatenate(
        [jnp.broadcast_to(aux[4:5, :], (8, width)), mask[...], jnp.broadcast_to(aux[5:6, :], (8, width))], 0
    )

    def lateral(x):
        return pltpu.roll(x, 1, 0) + pltpu.roll(x, total - 1, 0) + beside(x)

    d = ext[...]
    one0 = m * ((1.0 - 4.0 * h0 - v) * d + h0 * lateral(d))
    one1 = m * (v * d)
    two0 = (1.0 - 4.0 * h0 - v) * one0 + h0 * lateral(one0) + v * one1
    two1 = (1.0 - 4.0 * h1 - 2.0 * v) * one1 + h1 * lateral(one1) + v * one0
    two2 = v * one1
    for level, two in enumerate((two0, two1, two2)):
        three[level] = base[level] + (m * two)[8 : 8 + rows]
    copy = pltpu.make_async_copy(three, out.at[0, pl.ds(0, 3)], sem)
    copy.start()
    copy.wait()


def add_flux(base, back, mask, aux, whole):
    vmem = pl.BlockSpec(memory_space=pltpu.VMEM)
    hbm = pl.BlockSpec(memory_space=pltpu.HBM)
    rows, width = mask.shape
    return pl.pallas_call(
        add_kernel,
        out_shape=jax.ShapeDtypeStruct(whole.shape, jnp.float32),
        in_specs=[vmem, vmem, vmem, vmem, hbm],
        out_specs=hbm,
        scratch_shapes=[pltpu.VMEM((rows + 16, width), jnp.float32), pltpu.VMEM(base.shape, jnp.float32), pltpu.SemaphoreType.DMA],
        input_output_aliases={4: 0},
        compiler_params=pltpu.CompilerParams(vmem_limit_bytes=2 * MIB),
        cost_estimate=pl.CostEstimate(flops=30 * mask.size, bytes_accessed=32 * mask.size, transcendentals=0),
        name="add",
    )(base, back, mask, aux, whole)


def per_device(state, horiz_rate, vert_rate, sea_mask, exchange_coef, partner):
    ntile = lax.axis_size("tile")
    fields, hz, vt = state[0], horiz_rate[0], vert_rate[0]
    outgoing, scale = prep(fields, exchange_coef, sea_mask)
    got = lax.all_to_all(outgoing, BOTH, 0, 0, tiled=True)
    pieces = flux_pieces(partner, got)
    back = lax.all_to_all(pieces, BOTH, 0, 0, tiled=True)

    sent_near, sent_far = edges(fields, sea_mask)
    got_near = lax.ppermute(sent_near, "tile", [(i, i ^ 1) for i in range(ntile)])
    got_far = lax.ppermute(sent_far, "tile", [(i, (i + 2 * (i % 2) - 1) % ntile) for i in range(ntile)])
    whole, base, aux = mix(fields, hz, vt, sent_near, sent_far, got_near, got_far, scale)
    return add_flux(base, back, scale, aux, whole)[None]


def solution(mesh):
    placed = (
        P("comp", None, None, "tile", None),
        P("comp", None, None),
        P("comp", None),
        P("tile", None),
        P("tile", None),
        P(),
    )
    return jax.shard_map(
        per_device,
        mesh=mesh,
        in_specs=placed,
        out_specs=P("comp", None, None, "tile", None),
        check_vma=False,
    )
```

time: 45.1 us -> 42.6 us (0.945)
  Pallas kernels: 21.2 us -> 18.3 us
    pallas_call x2, Pallas kernels: 17.3 us -> 14.3 us  [the longest x1 12.6 us: mix(): pl.pallas_call(mix_kernel, out_shape=(jax.ShapeDtypeStruct(flat, jnp.floa...]
  transfers between devices with their start and end apart: 4 -> 4, of which waited for: 0 -> 0; matrix products, arithmetic and copies ran while one was open for 0% -> 0% of each run, Pallas kernels for 42% -> 37%
where the time goes in v4:
time: 42.6 us; the launch traced here: 42 us
  starting transfers between devices  23.6 us (55%)
  Pallas kernels  18.3 us (43%)
    pallas_call x1, Pallas kernels, mix(): pl.pallas_call(mix_kernel, out_shape=(jax.ShapeDtypeStruct(flat, jnp.floa...  12.6 us
    all_to_all x1, starting transfers between devices, per_device(): got = lax.all_to_all(outgoing, BOTH, 0, 0, tiled=True)  11.1 us
    ppermute x1, starting transfers between devices, per_device(): lax.ppermute(sent_far, 'tile', [(i, (i + 2 * (i % 2) - 1) % ntile) for i...  7.43 us
    all_to_all x1, starting transfers between devices, per_device(): back = lax.all_to_all(pieces, BOTH, 0, 0, tiled=True)  4.92 us
    pallas_call x1, Pallas kernels, edges(): pl.pallas_call(edge_kernel, out_shape=(shape, shape), in_specs=[hbm, anyw...  1.71 us
    pallas_call x1, Pallas kernels, prep(): pl.pallas_call(prep_kernel, out_shape=(jax.ShapeDtypeStruct((4 * rows, wi...  1.65 us
    pallas_call x1, Pallas kernels, flux_pieces(): pl.pallas_call(flux_kernel, out_shape=jax.ShapeDtypeStruct(got.shape, jnp...  1.32 us
    pallas_call x1, Pallas kernels, add_flux(): pl.pallas_call(add_kernel, out_shape=jax.ShapeDtypeStruct(whole.shape, jn...  0.95 us
  transfers between devices with their start and end apart: 4, of which 0 were waited for; matrix products, arithmetic and copies ran while one was open for 0% of the time, Pallas kernels for 37%

profile of v4, /device:TPU:0, one launch (start us, length us, event | category | flops | bytes accessed | tf_op | source)
XLA Modules:
  0.0 42.0 jit_solution(15117550569616987622)
XLA Ops:
  0.0 0.0 copy-start
  0.0 0.0 copy-start.4
  0.0 1.7 %prep.1 = (f32[256,128]{1,0:T(8,128)}, f32[64,256]{1,0:T(8,128)}) custom-call(f32[2,64,64,256]{3,2,1,0:T(8,128)} %bitcast.14, f32[64,256]{1,0:T(8,128)} %coef_hbm.1, s32[64,256]{1,0:T(8,128)} %sea_hbm.1), custom_call_target="tpu_custom_call" | custom-call | flops 49152 | bytes 393216 | tf_op jit(solution)/shard_map/prep/pallas_call | solution.py:274
  1.7 11.1 %all-to-all-start = ((f32[128,2,128]{2,1,0:T(2,128)}), f32[128,2,128]{2,1,0:T(2,128)S(1)}, u32[]{:S(2)}, u32[]{:S(2)}) async-start(f32[128,2,128]{2,1,0:T(2,128)} %bitcast.18), calls=%async_computation | async-start | bytes 262144 | tf_op jit(solution)/shard_map/all_to_all | solution.py:450
  12.8 0.0 copy-done
  12.8 1.7 %edges.1 = (f32[2,136,256]{2,1,0:T(8,128)S(1)}, f32[2,136,256]{2,1,0:T(8,128)S(1)}) custom-call(f32[2,64,64,256]{3,2,1,0:T(8,128)} %bitcast.15, s32[64,256]{1,0:T(8,128)S(1)} %copy-done), custom_call_target="tpu_custom_call" | custom-call | bytes 4194304 | tf_op jit(solution)/shard_map/edges/pallas_call | solution.py:338
  14.5 0.1 collective-permute-start
  14.6 7.4 %collective-permute-start.1 = (f32[2,136,256]{2,1,0:T(8,128)S(1)}, f32[2,136,256]{2,1,0:T(8,128)S(1)}, u32[]{:S(2)}, u32[]{:S(2)}) collective-permute-start(f32[2,136,256]{2,1,0:T(8,128)S(1)} %get-tuple-element.13.sent_far), channel_id=1, source_target_pairs={{0,63},{1,2},{2,1},{3,4},{4,3},{5,6},{6,5},{7,8},{8,7},{9,10},{10,... | collective-permute-start | bytes 835592 | tf_op jit(solution)/shard_map/ppermute | solution.py:456
  22.1 0.0 all-to-all-done
  22.1 0.0 copy-done.4
  22.1 0.0 copy-start.1
  22.1 0.0 copy-start.2
  22.1 0.0 copy-start.3
  22.1 1.3 %flux.1 = f32[256,128]{1,0:T(8,128)} custom-call(s32[64]{0:T(128)S(1)} %copy-done.4, f32[256,128]{1,0:T(8,128)S(1)} %bitcast.11), custom_call_target="tpu_custom_call" | custom-call | flops 30000001024 | bytes 262144 | tf_op jit(solution)/shard_map/flux/pallas_call | solution.py:375
  23.4 4.9 %all-to-all-start.1 = ((f32[128,2,128]{2,1,0:T(2,128)}), f32[128,2,128]{2,1,0:T(2,128)S(1)}, u32[]{:S(2)}, u32[]{:S(2)}) async-start(f32[128,2,128]{2,1,0:T(2,128)} %bitcast.6), calls=%async_computation.1 | async-start | bytes 262144 | tf_op jit(solution)/shard_map/all_to_all | solution.py:452
  28.3 0.0 collective-permute-done.got_near
  28.4 0.0 collective-permute-done.1.got_far
  28.4 0.0 copy-done.1
  28.4 0.0 copy-done.2
  28.4 0.0 copy-done.3
  28.4 12.6 %mix.1 = (f32[128,64,256]{2,1,0:T(8,128)}, f32[3,64,256]{2,1,0:T(8,128)S(1)}, f32[8,256]{1,0:T(8,128)S(1)}) custom-call(f32[2,64]{1,0:T(2,128)S(1)} %bitcast.12, f32[2]{0:T(128)S(1)} %bitcast.13, f32[128,64,256]{2,1,0:T(8,128)} %bitcast.16, f32[2,136,256]{2,1,0:T(8,128)S(1)} %get-tuple-element.12.sent_near, f32[2,136,256]{2,1,0:T(8,128)S(1)} %get-tuple-element.13.sent_far, ...), custom_call_target="tpu_custom_call" | custom-call | flops 54525952 | bytes 16777216 | tf_op jit(solution)/shard_map/mix/pallas_call | solution.py:214
  41.0 0.0 all-to-all-done.1
  41.0 1.0 %add.1 = f32[2,64,64,256]{3,2,1,0:T(8,128)} custom-call(f32[3,64,256]{2,1,0:T(8,128)S(1)} %get-tuple-element.15.base, f32[256,128]{1,0:T(8,128)S(1)} %bitcast.10, f32[64,256]{1,0:T(8,128)S(1)} %copy-done.1, f32[8,256]{1,0:T(8,128)S(1)} %get-tuple-element.17.aux, f32[2,64,64,256]{3,2,1,0:T(8,128)} %bitcast.17), custom_call_target="tpu_custom_call", output_to_operand_aliasing={{}: (4, {})} | custom-call | flops 491520 | bytes 524288 | tf_op jit(solution)/shard_map/add/pallas_call | solution.py:433
Async XLA Ops:
  0.0 12.8 %copy-start = (s32[64,256]{1,0:T(8,128)S(1)}, s32[64,256]{1,0:T(8,128)}, u32[]{:S(2)}) copy-start(s32[64,256]{1,0:T(8,128)} %sea_hbm.1) | copy-start | bytes 196612
  0.0 22.1 %copy-start.4 = (s32[64]{0:T(128)S(1)}, s32[64]{0:T(128)}, u32[]{:S(2)}) copy-start(s32[64]{0:T(128)} %partner.1) | copy-start | bytes 772
  1.7 20.4 %all-to-all-start = ((f32[128,2,128]{2,1,0:T(2,128)}), f32[128,2,128]{2,1,0:T(2,128)S(1)}, u32[]{:S(2)}, u32[]{:S(2)}) async-start(f32[128,2,128]{2,1,0:T(2,128)} %bitcast.18), calls=%async_computation | async-start | bytes 262144 | tf_op jit(solution)/shard_map/all_to_all | solution.py:450
  14.5 13.8 %collective-permute-start = (f32[2,136,256]{2,1,0:T(8,128)S(1)}, f32[2,136,256]{2,1,0:T(8,128)S(1)}, u32[]{:S(2)}, u32[]{:S(2)}) collective-permute-start(f32[2,136,256]{2,1,0:T(8,128)S(1)} %get-tuple-element.12.sent_near), channel_id=1, source_target_pairs={{0,1},{1,0},{2,3},{3,2},{4,5},{5,4},{6,7},{7,6},{8,9},{9,8},{10,11... | collective-permute-start | bytes 835592 | tf_op jit(solution)/shard_map/ppermute | solution.py:455
  14.6 13.7 %collective-permute-start.1 = (f32[2,136,256]{2,1,0:T(8,128)S(1)}, f32[2,136,256]{2,1,0:T(8,128)S(1)}, u32[]{:S(2)}, u32[]{:S(2)}) collective-permute-start(f32[2,136,256]{2,1,0:T(8,128)S(1)} %get-tuple-element.13.sent_far), channel_id=1, source_target_pairs={{0,63},{1,2},{2,1},{3,4},{4,3},{5,6},{6,5},{7,8},{8,7},{9,10},{10,... | collective-permute-start | bytes 835592 | tf_op jit(solution)/shard_map/ppermute | solution.py:456
  22.1 6.3 %copy-start.1 = (f32[64,256]{1,0:T(8,128)S(1)}, f32[64,256]{1,0:T(8,128)}, u32[]{:S(2)}) copy-start(f32[64,256]{1,0:T(8,128)} %get-tuple-element.14.mask) | copy-start | bytes 196612
  22.1 6.3 %copy-start.2 = (f32[1,2,64]{2,1,0:T(2,128)S(1)}, f32[1,2,64]{2,1,0:T(2,128)}, u32[]{:S(2)}) copy-start(f32[1,2,64]{2,1,0:T(2,128)} %param.7) | copy-start | bytes 1540
  22.1 6.3 %copy-start.3 = (f32[1,2]{1,0:T(1,128)S(1)}, f32[1,2]{1,0:T(1,128)}, u32[]{:S(2)}) copy-start(f32[1,2]{1,0:T(1,128)} %param.8) | copy-start | bytes 28
  23.4 17.6 %all-to-all-start.1 = ((f32[128,2,128]{2,1,0:T(2,128)}), f32[128,2,128]{2,1,0:T(2,128)S(1)}, u32[]{:S(2)}, u32[]{:S(2)}) async-start(f32[128,2,128]{2,1,0:T(2,128)} %bitcast.6), calls=%async_computation.1 | async-start | bytes 262144 | tf_op jit(solution)/shard_map/all_to_all | solution.py:452

commit v5 on v4

--- a/solution.py
+++ b/solution.py
@@ -8,7 +8,6 @@
 from jax.sharding import PartitionSpec as P
 
 BOTH = ("comp", "tile")
-CHUNK = 8
 BLOCK = 16
 MIB = 1 << 20
 
@@ -35,23 +34,31 @@
 ):
     planes, rows, width = state.shape
     fields, levels = hz.shape
-    total = planes // CHUNK
+    blocks = planes // BLOCK
     half = width // 2
     sides = [pl.ds(k * half, half) for k in range(2)]
 
-    def load(q):
-        at = pl.ds(q * CHUNK, CHUNK)
+    def load(at, q):
         return [
             pltpu.make_async_copy(state.at[at, :, lanes], raw.at[k, at], in_sem.at[q, k])
             for k, lanes in enumerate(sides)
         ]
 
-    def store(q):
-        at = pl.ds(q * CHUNK, CHUNK)
+    def store(at):
         return [
-            pltpu.make_async_copy(res.at[k, at], out.at[at, :, lanes], out_sem.at[q, k])
+            pltpu.make_async_copy(res.at[k, at], out.at[at, :, lanes], out_sem.at[k])
             for k, lanes in enumerate(sides)
         ]
+
+    def ready(q):
+        if isinstance(q, int):
+            lo, hi = q * BLOCK + (q > 0), min((q + 1) * BLOCK + 1, planes)
+            return load(pl.ds(lo, hi - lo), q)
+        return load(pl.ds(q * BLOCK + 1, BLOCK), q)
+
+    def leave(lo, count):
+        for copy in store(pl.ds(lo, count)):
+            copy.start()
 
     odd = lax.axis_index("tile") % 2
     strips = [
@@ -66,9 +73,8 @@
     for copy in rates:
         copy.start()
 
-    @pl.loop(0, total)
-    def _(q):
-        for copy in load(q):
+    for q in range(blocks):
+        for copy in ready(q):
             copy.start()
 
     for copy in rates:
@@ -149,28 +155,23 @@
         hi = p + 1 if i else jnp.where(p % levels == levels - 1, p, p + 1)
         second_at(p, lo, hi)
 
-    blocks, step = planes // BLOCK, BLOCK // CHUNK
-
-    def arrive(q):
-        for copy in load(q):
-            copy.wait()
-
-    def leave(q):
-        for copy in store(q):
-            copy.start()
-
-    for j in range(step + 1):
-        arrive(j)
+    for copy in ready(0):
+        copy.wait()
     pack(0)
     for i in range(BLOCK):
         first(0, i)
 
     @pl.loop(1, blocks)
     def _(q):
-        for j in range(1, step + 1):
-            @pl.when(q * step + j < total)
-            def _(j=j):
-                arrive(q * step + j)
+        @pl.when(q < blocks - 1)
+        def _():
+            for copy in ready(q):
+                copy.wait()
+
+        @pl.when(q == blocks - 1)
+        def _():
+            for copy in ready(blocks - 1):
+                copy.wait()
 
         now = q * BLOCK
         for i in range(BLOCK):
@@ -180,27 +181,24 @@
 
         @pl.when(q > 1)
         def _():
-            leave((q - 1) * step - 1)
-
-        for j in range(step - 1):
-            leave((q - 1) * step + j)
+            leave(now - BLOCK - 1, BLOCK)
 
         @pl.when(q == 1)
         def _():
+            leave(0, BLOCK - 1)
             for k, lanes in enumerate(sides):
                 base[:, :, lanes] = res[k, 0:3]
 
+    done = planes - BLOCK - 1
     for i in range(BLOCK):
         second(planes - BLOCK, i)
-        if i % CHUNK == 0:
-            leave(total - step - 1 + i // CHUNK)
+        if i == BLOCK // 2:
+            leave(done, i + 1)
+            done += i + 1
     second_at(planes - 1, planes - 2, planes - 1)
-    leave(total - 1)
-
-    @pl.loop(0, total)
-    def _(q):
-        for copy in store(q):
-            copy.wait()
+    leave(done, planes - done)
+    for copy in store(pl.ds(0, planes)):
+        copy.wait()
 
 
 def mix(fields, hz, vt, sent_near, sent_far, got_near, got_far, mask):
@@ -209,7 +207,7 @@
     flat = (planes, rows, width)
     vmem = pl.BlockSpec(memory_space=pltpu.VMEM)
     hbm = pl.BlockSpec(memory_space=pltpu.HBM)
-    total = nf * levels // CHUNK
+    blocks = planes // BLOCK
     halved = (2, planes, rows, width // 2)
     whole, base, aux = pl.pallas_call(
         mix_kernel,
@@ -235,8 +233,8 @@
             pltpu.VMEM((2, rows, width // 2), jnp.float32),
             pltpu.VMEM((rows, width), jnp.float32),
             pltpu.SemaphoreType.DMA((2,)),
-            pltpu.SemaphoreType.DMA((total, 2)),
-            pltpu.SemaphoreType.DMA((total, 2)),
+            pltpu.SemaphoreType.DMA((blocks, 2)),
+            pltpu.SemaphoreType.DMA((2,)),
         ],
         compiler_params=pltpu.CompilerParams(vmem_limit_bytes=46 * MIB),
         cost_estimate=pl.CostEstimate(flops=26 * fields.size, bytes_accessed=8 * fields.size, transcendentals=0),
@@ -291,7 +289,7 @@
     )(fields, coef, sea)
 
 
-def edge_kernel(state, sea_any, near, far, stage, sea, sem):
+def edge_kernel(state, sea_any, partner_any, near, far, chosen, stage, sea, partner, sem):
     nf, levels, rows, width = state.shape
     planes = nf * levels
     copies = [
@@ -299,11 +297,18 @@
         for side, at in enumerate((0, rows - 8))
         for f in range(nf)
     ]
-    mask_copy = pltpu.make_async_copy(sea_any, sea, sem.at[2, 0])
-    mask_copy.start()
-    for copy in copies:
+    small = [
+        pltpu.make_async_copy(sea_any, sea, sem.at[2, 0]),
+        pltpu.make_async_copy(partner_any, partner, sem.at[2, 1]),
+    ]
+    for copy in small + copies:
         copy.start()
-    mask_copy.wait()
+    for copy in small:
+        copy.wait()
+    tiles = chosen.shape[0]
+    column = lax.broadcasted_iota(jnp.int32, (1, tiles), 1)
+    for t in range(tiles):
+        chosen[t : t + 1, :] = (column == partner[t]).astype(jnp.float32)
 
     def fill(first, last):
         for side, (out, at) in enumerate(((first, 0), (last, 6))):
@@ -329,7 +334,7 @@
         fill(near, far)
 
 
-def edges(fields, sea):
+def edges(fields, sea, partner):
     vmem = pl.BlockSpec(memory_space=pltpu.VMEM)
     anyw = pl.BlockSpec(memory_space=pl.ANY)
     hbm = pl.BlockSpec(memory_space=pltpu.HBM)
@@ -337,30 +342,30 @@
     shape = jax.ShapeDtypeStruct((2, nf * levels + 8, width), jnp.float32)
     return pl.pallas_call(
         edge_kernel,
-        out_shape=(shape, shape),
-        in_specs=[hbm, anyw],
-        out_specs=(vmem, vmem),
+        out_shape=(shape, shape, jax.ShapeDtypeStruct((partner.size, partner.size), jnp.float32)),
+        in_specs=[hbm, anyw, anyw],
+        out_specs=(vmem, vmem, vmem),
         scratch_shapes=[
             pltpu.VMEM((2, nf, levels, 8, width), jnp.float32),
             pltpu.VMEM(sea.shape, jnp.int32),
+            pltpu.SMEM(partner.shape, jnp.int32),
             pltpu.SemaphoreType.DMA((3, nf)),
         ],
         compiler_params=pltpu.CompilerParams(vmem_limit_bytes=46 * MIB),
         cost_estimate=pl.CostEstimate(flops=0, bytes_accessed=4 * MIB, transcendentals=0),
         name="edges",
-    )(fields, sea)
-
-
-def flux_kernel(partner, got, back, theirs, mine, other):
-    tiles = got.shape[0] // 4
-    for t in range(tiles):
-        theirs[2 * t : 2 * t + 2, :] = got[pl.ds(2 * tiles + 2 * partner[t], 2), :]
+    )(fields, sea, partner)
+
+
+def flux_kernel(chosen, got, back):
+    tiles, half = chosen.shape[0], got.shape[1]
     odd, even = pl.ds(1, tiles, stride=2), pl.ds(0, tiles, stride=2)
-    flux = got[odd, :] * (got[even, :] - theirs[even, :]) * theirs[odd, :]
-    mine[...] = flux
-    for t in range(tiles):
-        other[pl.ds(partner[t], 1), :] = mine[t : t + 1, :]
-    turned = other[...]
+    ocean = jnp.concatenate([got[pl.ds(2 * tiles + k, tiles, stride=2), :] for k in range(2)], 1)
+    theirs = jnp.dot(chosen[...], ocean, precision=lax.Precision.HIGHEST, preferred_element_type=jnp.float32)
+    flux = got[odd, :] * (got[even, :] - theirs[:, 0:half]) * theirs[:, half:]
+    turned = lax.dot_general(
+        chosen[...], flux, (((0,), (0,)), ((), ())), precision=lax.Precision.HIGHEST, preferred_element_type=jnp.float32
+    )
     shift = jnp.where(lax.axis_index("tile") < 2, tiles - 1, 1)
     back[even, :] = flux
     back[odd, :] = pltpu.roll(flux, shift, 0)
@@ -368,24 +373,17 @@
     back[pl.ds(2 * tiles + 1, tiles, stride=2), :] = pltpu.roll(turned, shift, 0)
 
 
-def flux_pieces(partner, got):
+def flux_pieces(chosen, got):
     vmem = pl.BlockSpec(memory_space=pltpu.VMEM)
-    smem = pl.BlockSpec(memory_space=pltpu.SMEM)
-    tiles, half = got.shape[0] // 4, got.shape[1]
     return pl.pallas_call(
         flux_kernel,
         out_shape=jax.ShapeDtypeStruct(got.shape, jnp.float32),
-        in_specs=[smem, vmem],
+        in_specs=[vmem, vmem],
         out_specs=vmem,
-        scratch_shapes=[
-            pltpu.VMEM((2 * tiles, half), jnp.float32),
-            pltpu.VMEM((tiles, half), jnp.float32),
-            pltpu.VMEM((tiles, half), jnp.float32),
-        ],
         compiler_params=pltpu.CompilerParams(vmem_limit_bytes=2 * MIB),
         cost_estimate=pl.CostEstimate(flops=3 * 10**10, bytes_accessed=8 * got.size, transcendentals=0),
         name="flux",
-    )(partner, got)
+    )(chosen, got)
 
 
 def add_kernel(base, back, mask, aux, whole, out, ext, three, sem):
@@ -448,10 +446,10 @@
     fields, hz, vt = state[0], horiz_rate[0], vert_rate[0]
     outgoing, scale = prep(fields, exchange_coef, sea_mask)
     got = lax.all_to_all(outgoing, BOTH, 0, 0, tiled=True)
-    pieces = flux_pieces(partner, got)
+    sent_near, sent_far, chosen = edges(fields, sea_mask, partner)
+    pieces = flux_pieces(chosen, got)
     back = lax.all_to_all(pieces, BOTH, 0, 0, tiled=True)
 
-    sent_near, sent_far = edges(fields, sea_mask)
     got_near = lax.ppermute(sent_near, "tile", [(i, i ^ 1) for i in range(ntile)])
     got_far = lax.ppermute(sent_far, "tile", [(i, (i + 2 * (i % 2) - 1) % ntile) for i in range(ntile)])
     whole, base, aux = mix(fields, hz, vt, sent_near, sent_far, got_near, got_far, scale)

time: 42.6 us -> 41.8 us (0.981)
  Pallas kernels: 18.3 us -> 17.4 us
    pallas_call x1, Pallas kernels: 12.6 us -> 12.1 us  [mix(): pl.pallas_call(mix_kernel, out_shape=(jax.ShapeDtypeStruct(flat, jnp.floa...]
  transfers between devices with their start and end apart: 4 -> 4, of which waited for: 0 -> 0; matrix products, arithmetic and copies ran while one was open for 0% -> 0% of each run, Pallas kernels for 37% -> 36%
where the time goes in v5:
time: 41.8 us; the launch traced here: 41.2 us
  starting transfers between devices  23.6 us (56%)
  Pallas kernels  17.4 us (42%)
    pallas_call x1, Pallas kernels, mix(): pl.pallas_call(mix_kernel, out_shape=(jax.ShapeDtypeStruct(flat, jnp.floa...  12.1 us
    all_to_all x1, starting transfers between devices, per_device(): got = lax.all_to_all(outgoing, BOTH, 0, 0, tiled=True)  11.1 us
    ppermute x1, starting transfers between devices, per_device(): lax.ppermute(sent_far, 'tile', [(i, (i + 2 * (i % 2) - 1) % ntile) for i...  7.43 us
    all_to_all x1, starting transfers between devices, per_device(): back = lax.all_to_all(pieces, BOTH, 0, 0, tiled=True)  4.92 us
    pallas_call x1, Pallas kernels, edges(): pl.pallas_call(edge_kernel, out_shape=(shape, shape, jax.ShapeDtypeStruct...  1.71 us
    pallas_call x1, Pallas kernels, prep(): pl.pallas_call(prep_kernel, out_shape=(jax.ShapeDtypeStruct((4 * rows, wi...  1.65 us
    pallas_call x1, Pallas kernels, flux_pieces(): pl.pallas_call(flux_kernel, out_shape=jax.ShapeDtypeStruct(got.shape, jnp...  1.05 us
    pallas_call x1, Pallas kernels, add_flux(): pl.pallas_call(add_kernel, out_shape=jax.ShapeDtypeStruct(whole.shape, jn...  0.95 us
  transfers between devices with their start and end apart: 4, of which 0 were waited for; matrix products, arithmetic and copies ran while one was open for 0% of the time, Pallas kernels for 36%

profile of v5, /device:TPU:0, one launch (start us, length us, event | category | flops | bytes accessed | tf_op | source)
XLA Modules:
  0.0 41.2 jit_solution(9182508724118456873)
XLA Ops:
  0.0 0.0 copy-start
  0.0 0.0 copy-start.3
  0.0 1.7 %prep.1 = (f32[256,128]{1,0:T(8,128)}, f32[64,256]{1,0:T(8,128)}) custom-call(f32[2,64,64,256]{3,2,1,0:T(8,128)} %bitcast.14, f32[64,256]{1,0:T(8,128)} %coef_hbm.1, s32[64,256]{1,0:T(8,128)} %sea_hbm.1), custom_call_target="tpu_custom_call" | custom-call | flops 49152 | bytes 393216 | tf_op jit(solution)/shard_map/prep/pallas_call | solution.py:272
  1.7 11.1 %all-to-all-start = ((f32[128,2,128]{2,1,0:T(2,128)}), f32[128,2,128]{2,1,0:T(2,128)S(1)}, u32[]{:S(2)}, u32[]{:S(2)}) async-start(f32[128,2,128]{2,1,0:T(2,128)} %bitcast.18), calls=%async_computation | async-start | bytes 262144 | tf_op jit(solution)/shard_map/all_to_all | solution.py:448
  12.8 0.0 copy-done
  12.8 0.0 copy-done.3
  12.8 1.7 %edges.1 = (f32[2,136,256]{2,1,0:T(8,128)S(1)}, f32[2,136,256]{2,1,0:T(8,128)S(1)}, f32[64,64]{1,0:T(8,128)S(1)}) custom-call(f32[2,64,64,256]{3,2,1,0:T(8,128)} %bitcast.15, s32[64,256]{1,0:T(8,128)S(1)} %copy-done, s32[64]{0:T(128)S(1)} %copy-done.3), custom_call_target="tpu_custom_call" | custom-call | bytes 4194304 | tf_op jit(solution)/shard_map/edges/pallas_call | solution.py:343
  14.6 0.1 collective-permute-start
  14.7 7.4 %collective-permute-start.1 = (f32[2,136,256]{2,1,0:T(8,128)S(1)}, f32[2,136,256]{2,1,0:T(8,128)S(1)}, u32[]{:S(2)}, u32[]{:S(2)}) collective-permute-start(f32[2,136,256]{2,1,0:T(8,128)S(1)} %get-tuple-element.14.sent_far), channel_id=1, source_target_pairs={{0,63},{1,2},{2,1},{3,4},{4,3},{5,6},{6,5},{7,8},{8,7},{9,10},{10,... | collective-permute-start | bytes 835592 | tf_op jit(solution)/shard_map/ppermute | solution.py:454
  22.1 0.0 all-to-all-done
  22.1 0.0 copy-start.1
  22.1 0.0 copy-start.2
  22.1 0.0 copy-start.4
  22.1 1.0 %flux.1 = f32[256,128]{1,0:T(8,128)} custom-call(f32[64,64]{1,0:T(8,128)S(1)} %get-tuple-element.17.chosen, f32[256,128]{1,0:T(8,128)S(1)} %bitcast.11), custom_call_target="tpu_custom_call" | custom-call | flops 30000001024 | bytes 262144 | tf_op jit(solution)/shard_map/flux/pallas_call | solution.py:378
  23.1 4.9 %all-to-all-start.1 = ((f32[128,2,128]{2,1,0:T(2,128)}), f32[128,2,128]{2,1,0:T(2,128)S(1)}, u32[]{:S(2)}, u32[]{:S(2)}) async-start(f32[128,2,128]{2,1,0:T(2,128)} %bitcast.6), calls=%async_computation.1 | async-start | bytes 262144 | tf_op jit(solution)/shard_map/all_to_all | solution.py:451
  28.1 0.0 collective-permute-done.got_near
  28.1 0.0 collective-permute-done.1.got_far
  28.1 0.0 copy-done.1
  28.1 0.0 copy-done.2
  28.1 0.0 copy-done.4
  28.1 12.1 %mix.1 = (f32[128,64,256]{2,1,0:T(8,128)}, f32[3,64,256]{2,1,0:T(8,128)S(1)}, f32[8,256]{1,0:T(8,128)S(1)}) custom-call(f32[2,64]{1,0:T(2,128)S(1)} %bitcast.12, f32[2]{0:T(128)S(1)} %bitcast.13, f32[128,64,256]{2,1,0:T(8,128)} %bitcast.16, f32[2,136,256]{2,1,0:T(8,128)S(1)} %get-tuple-element.13.sent_near, f32[2,136,256]{2,1,0:T(8,128)S(1)} %get-tuple-element.14.sent_far, ...), custom_call_target="tpu_custom_call" | custom-call | flops 54525952 | bytes 16777216 | tf_op jit(solution)/shard_map/mix/pallas_call | solution.py:212
  40.2 0.0 all-to-all-done.1
  40.2 1.0 %add.1 = f32[2,64,64,256]{3,2,1,0:T(8,128)} custom-call(f32[3,64,256]{2,1,0:T(8,128)S(1)} %get-tuple-element.16.base, f32[256,128]{1,0:T(8,128)S(1)} %bitcast.10, f32[64,256]{1,0:T(8,128)S(1)} %copy-done.1, f32[8,256]{1,0:T(8,128)S(1)} %get-tuple-element.19.aux, f32[2,64,64,256]{3,2,1,0:T(8,128)} %bitcast.17), custom_call_target="tpu_custom_call", output_to_operand_aliasing={{}: (4, {})} | custom-call | flops 491520 | bytes 524288 | tf_op jit(solution)/shard_map/add/pallas_call | solution.py:431
Async XLA Ops:
  0.0 12.8 %copy-start = (s32[64,256]{1,0:T(8,128)S(1)}, s32[64,256]{1,0:T(8,128)}, u32[]{:S(2)}) copy-start(s32[64,256]{1,0:T(8,128)} %sea_hbm.1) | copy-start | bytes 196612
  0.0 12.8 %copy-start.3 = (s32[64]{0:T(128)S(1)}, s32[64]{0:T(128)}, u32[]{:S(2)}) copy-start(s32[64]{0:T(128)} %partner_any.1) | copy-start | bytes 772
  1.7 20.4 %all-to-all-start = ((f32[128,2,128]{2,1,0:T(2,128)}), f32[128,2,128]{2,1,0:T(2,128)S(1)}, u32[]{:S(2)}, u32[]{:S(2)}) async-start(f32[128,2,128]{2,1,0:T(2,128)} %bitcast.18), calls=%async_computation | async-start | bytes 262144 | tf_op jit(solution)/shard_map/all_to_all | solution.py:448
  14.6 13.5 %collective-permute-start = (f32[2,136,256]{2,1,0:T(8,128)S(1)}, f32[2,136,256]{2,1,0:T(8,128)S(1)}, u32[]{:S(2)}, u32[]{:S(2)}) collective-permute-start(f32[2,136,256]{2,1,0:T(8,128)S(1)} %get-tuple-element.13.sent_near), channel_id=1, source_target_pairs={{0,1},{1,0},{2,3},{3,2},{4,5},{5,4},{6,7},{7,6},{8,9},{9,8},{10,11... | collective-permute-start | bytes 835592 | tf_op jit(solution)/shard_map/ppermute | solution.py:453
  14.7 13.4 %collective-permute-start.1 = (f32[2,136,256]{2,1,0:T(8,128)S(1)}, f32[2,136,256]{2,1,0:T(8,128)S(1)}, u32[]{:S(2)}, u32[]{:S(2)}) collective-permute-start(f32[2,136,256]{2,1,0:T(8,128)S(1)} %get-tuple-element.14.sent_far), channel_id=1, source_target_pairs={{0,63},{1,2},{2,1},{3,4},{4,3},{5,6},{6,5},{7,8},{8,7},{9,10},{10,... | collective-permute-start | bytes 835592 | tf_op jit(solution)/shard_map/ppermute | solution.py:454
  22.1 6.0 %copy-start.1 = (f32[64,256]{1,0:T(8,128)S(1)}, f32[64,256]{1,0:T(8,128)}, u32[]{:S(2)}) copy-start(f32[64,256]{1,0:T(8,128)} %get-tuple-element.15.mask) | copy-start | bytes 196612
  22.1 6.0 %copy-start.2 = (f32[1,2,64]{2,1,0:T(2,128)S(1)}, f32[1,2,64]{2,1,0:T(2,128)}, u32[]{:S(2)}) copy-start(f32[1,2,64]{2,1,0:T(2,128)} %param.7) | copy-start | bytes 1540
  22.1 6.0 %copy-start.4 = (f32[1,2]{1,0:T(1,128)S(1)}, f32[1,2]{1,0:T(1,128)}, u32[]{:S(2)}) copy-start(f32[1,2]{1,0:T(1,128)} %param.8) | copy-start | bytes 28
  23.1 17.1 %all-to-all-start.1 = ((f32[128,2,128]{2,1,0:T(2,128)}), f32[128,2,128]{2,1,0:T(2,128)S(1)}, u32[]{:S(2)}, u32[]{:S(2)}) async-start(f32[128,2,128]{2,1,0:T(2,128)} %bitcast.6), calls=%async_computation.1 | async-start | bytes 262144 | tf_op jit(solution)/shard_map/all_to_all | solution.py:451

commit v6 on v5

--- a/solution.py
+++ b/solution.py
@@ -8,7 +8,8 @@
 from jax.sharding import PartitionSpec as P
 
 BOTH = ("comp", "tile")
-BLOCK = 16
+BLOCK = 32
+PART = 16
 MIB = 1 << 20
 
 
@@ -52,9 +53,9 @@
 
     def ready(q):
         if isinstance(q, int):
-            lo, hi = q * BLOCK + (q > 0), min((q + 1) * BLOCK + 1, planes)
+            lo, hi = q * PART + (q > 0), min((q + 1) * PART + 1, planes)
             return load(pl.ds(lo, hi - lo), q)
-        return load(pl.ds(q * BLOCK + 1, BLOCK), q)
+        return load(pl.ds(q * PART + 1, PART), q)
 
     def leave(lo, count):
         for copy in store(pl.ds(lo, count)):
@@ -73,7 +74,8 @@
     for copy in rates:
         copy.start()
 
-    for q in range(blocks):
+    parts = planes // PART
+    for q in range(parts):
         for copy in ready(q):
             copy.start()
 
@@ -159,18 +161,25 @@
         copy.wait()
     pack(0)
     for i in range(BLOCK):
+        if i and i % PART == 0:
+            for copy in ready(i // PART):
+                copy.wait()
         first(0, i)
 
     @pl.loop(1, blocks)
     def _(q):
+        for j in range(BLOCK // PART - 1):
+            for copy in ready(q * (BLOCK // PART) + j):
+                copy.wait()
+
         @pl.when(q < blocks - 1)
         def _():
-            for copy in ready(q):
+            for copy in ready((q + 1) * (BLOCK // PART) - 1):
                 copy.wait()
 
         @pl.when(q == blocks - 1)
         def _():
-            for copy in ready(blocks - 1):
+            for copy in ready(parts - 1):
                 copy.wait()
 
         now = q * BLOCK
@@ -192,9 +201,9 @@
     done = planes - BLOCK - 1
     for i in range(BLOCK):
         second(planes - BLOCK, i)
-        if i == BLOCK // 2:
-            leave(done, i + 1)
-            done += i + 1
+        if i in (BLOCK // 2, 3 * BLOCK // 4):
+            leave(done, planes - BLOCK + i - done)
+            done = planes - BLOCK + i
     second_at(planes - 1, planes - 2, planes - 1)
     leave(done, planes - done)
     for copy in store(pl.ds(0, planes)):
@@ -207,7 +216,6 @@
     flat = (planes, rows, width)
     vmem = pl.BlockSpec(memory_space=pltpu.VMEM)
     hbm = pl.BlockSpec(memory_space=pltpu.HBM)
-    blocks = planes // BLOCK
     halved = (2, planes, rows, width // 2)
     whole, base, aux = pl.pallas_call(
         mix_kernel,
@@ -233,7 +241,7 @@
             pltpu.VMEM((2, rows, width // 2), jnp.float32),
             pltpu.VMEM((rows, width), jnp.float32),
             pltpu.SemaphoreType.DMA((2,)),
-            pltpu.SemaphoreType.DMA((blocks, 2)),
+            pltpu.SemaphoreType.DMA((planes // PART, 2)),
             pltpu.SemaphoreType.DMA((2,)),
         ],
         compiler_params=pltpu.CompilerParams(vmem_limit_bytes=46 * MIB),

time: 41.8 us -> 41.4 us (level)
  transfers between devices with their start and end apart: 4 -> 4, of which waited for: 0 -> 0; matrix products, arithmetic and copies ran while one was open for 0% -> 0% of each run, Pallas kernels for 36% -> 35%
where the time goes in v6:
time: 41.4 us; the launch traced here: 40.8 us
  starting transfers between devices  23.6 us (57%)
  Pallas kernels  17.1 us (41%)
    pallas_call x1, Pallas kernels, mix(): pl.pallas_call(mix_kernel, out_shape=(jax.ShapeDtypeStruct(flat, jnp.floa...  11.7 us
    all_to_all x1, starting transfers between devices, per_device(): got = lax.all_to_all(outgoing, BOTH, 0, 0, tiled=True)  11.1 us
    ppermute x1, starting transfers between devices, per_device(): lax.ppermute(sent_far, 'tile', [(i, (i + 2 * (i % 2) - 1) % ntile) for i...  7.43 us
    all_to_all x1, starting transfers between devices, per_device(): back = lax.all_to_all(pieces, BOTH, 0, 0, tiled=True)  4.92 us
    pallas_call x1, Pallas kernels, edges(): pl.pallas_call(edge_kernel, out_shape=(shape, shape, jax.ShapeDtypeStruct...  1.71 us
    pallas_call x1, Pallas kernels, prep(): pl.pallas_call(prep_kernel, out_shape=(jax.ShapeDtypeStruct((4 * rows, wi...  1.65 us
    pallas_call x1, Pallas kernels, flux_pieces(): pl.pallas_call(flux_kernel, out_shape=jax.ShapeDtypeStruct(got.shape, jnp...  1.05 us
    pallas_call x1, Pallas kernels, add_flux(): pl.pallas_call(add_kernel, out_shape=jax.ShapeDtypeStruct(whole.shape, jn...  0.95 us
  transfers between devices with their start and end apart: 4, of which 0 were waited for; matrix products, arithmetic and copies ran while one was open for 0% of the time, Pallas kernels for 35%

profile of v6, /device:TPU:0, one launch (start us, length us, event | category | flops | bytes accessed | tf_op | source)
XLA Modules:
  0.0 40.8 jit_solution(16100315869787255395)
XLA Ops:
  0.0 0.0 copy-start
  0.0 0.0 copy-start.3
  0.0 1.7 %prep.1 = (f32[256,128]{1,0:T(8,128)}, f32[64,256]{1,0:T(8,128)}) custom-call(f32[2,64,64,256]{3,2,1,0:T(8,128)} %bitcast.14, f32[64,256]{1,0:T(8,128)} %coef_hbm.1, s32[64,256]{1,0:T(8,128)} %sea_hbm.1), custom_call_target="tpu_custom_call" | custom-call | flops 49152 | bytes 393216 | tf_op jit(solution)/shard_map/prep/pallas_call | solution.py:280
  1.7 11.1 %all-to-all-start = ((f32[128,2,128]{2,1,0:T(2,128)}), f32[128,2,128]{2,1,0:T(2,128)S(1)}, u32[]{:S(2)}, u32[]{:S(2)}) async-start(f32[128,2,128]{2,1,0:T(2,128)} %bitcast.18), calls=%async_computation | async-start | bytes 262144 | tf_op jit(solution)/shard_map/all_to_all | solution.py:456
  12.8 0.0 copy-done
  12.8 0.0 copy-done.3
  12.8 1.7 %edges.1 = (f32[2,136,256]{2,1,0:T(8,128)S(1)}, f32[2,136,256]{2,1,0:T(8,128)S(1)}, f32[64,64]{1,0:T(8,128)S(1)}) custom-call(f32[2,64,64,256]{3,2,1,0:T(8,128)} %bitcast.15, s32[64,256]{1,0:T(8,128)S(1)} %copy-done, s32[64]{0:T(128)S(1)} %copy-done.3), custom_call_target="tpu_custom_call" | custom-call | bytes 4194304 | tf_op jit(solution)/shard_map/edges/pallas_call | solution.py:351
  14.6 0.1 collective-permute-start
  14.7 7.4 %collective-permute-start.1 = (f32[2,136,256]{2,1,0:T(8,128)S(1)}, f32[2,136,256]{2,1,0:T(8,128)S(1)}, u32[]{:S(2)}, u32[]{:S(2)}) collective-permute-start(f32[2,136,256]{2,1,0:T(8,128)S(1)} %get-tuple-element.14.sent_far), channel_id=1, source_target_pairs={{0,63},{1,2},{2,1},{3,4},{4,3},{5,6},{6,5},{7,8},{8,7},{9,10},{10,... | collective-permute-start | bytes 835592 | tf_op jit(solution)/shard_map/ppermute | solution.py:462
  22.1 0.0 all-to-all-done
  22.1 0.0 copy-start.1
  22.1 0.0 copy-start.2
  22.1 0.0 copy-start.4
  22.1 1.0 %flux.1 = f32[256,128]{1,0:T(8,128)} custom-call(f32[64,64]{1,0:T(8,128)S(1)} %get-tuple-element.17.chosen, f32[256,128]{1,0:T(8,128)S(1)} %bitcast.11), custom_call_target="tpu_custom_call" | custom-call | flops 30000001024 | bytes 262144 | tf_op jit(solution)/shard_map/flux/pallas_call | solution.py:386
  23.1 4.9 %all-to-all-start.1 = ((f32[128,2,128]{2,1,0:T(2,128)}), f32[128,2,128]{2,1,0:T(2,128)S(1)}, u32[]{:S(2)}, u32[]{:S(2)}) async-start(f32[128,2,128]{2,1,0:T(2,128)} %bitcast.6), calls=%async_computation.1 | async-start | bytes 262144 | tf_op jit(solution)/shard_map/all_to_all | solution.py:459
  28.1 0.0 collective-permute-done.got_near
  28.1 0.0 collective-permute-done.1.got_far
  28.1 0.0 copy-done.1
  28.1 0.0 copy-done.2
  28.1 0.0 copy-done.4
  28.1 11.7 %mix.1 = (f32[128,64,256]{2,1,0:T(8,128)}, f32[3,64,256]{2,1,0:T(8,128)S(1)}, f32[8,256]{1,0:T(8,128)S(1)}) custom-call(f32[2,64]{1,0:T(2,128)S(1)} %bitcast.12, f32[2]{0:T(128)S(1)} %bitcast.13, f32[128,64,256]{2,1,0:T(8,128)} %bitcast.16, f32[2,136,256]{2,1,0:T(8,128)S(1)} %get-tuple-element.13.sent_near, f32[2,136,256]{2,1,0:T(8,128)S(1)} %get-tuple-element.14.sent_far, ...), custom_call_target="tpu_custom_call" | custom-call | flops 54525952 | bytes 16777216 | tf_op jit(solution)/shard_map/mix/pallas_call | solution.py:220
  39.8 0.0 all-to-all-done.1
  39.9 1.0 %add.1 = f32[2,64,64,256]{3,2,1,0:T(8,128)} custom-call(f32[3,64,256]{2,1,0:T(8,128)S(1)} %get-tuple-element.16.base, f32[256,128]{1,0:T(8,128)S(1)} %bitcast.10, f32[64,256]{1,0:T(8,128)S(1)} %copy-done.1, f32[8,256]{1,0:T(8,128)S(1)} %get-tuple-element.19.aux, f32[2,64,64,256]{3,2,1,0:T(8,128)} %bitcast.17), custom_call_target="tpu_custom_call", output_to_operand_aliasing={{}: (4, {})} | custom-call | flops 491520 | bytes 524288 | tf_op jit(solution)/shard_map/add/pallas_call | solution.py:439
Async XLA Ops:
  0.0 12.8 %copy-start = (s32[64,256]{1,0:T(8,128)S(1)}, s32[64,256]{1,0:T(8,128)}, u32[]{:S(2)}) copy-start(s32[64,256]{1,0:T(8,128)} %sea_hbm.1) | copy-start | bytes 196612
  0.0 12.8 %copy-start.3 = (s32[64]{0:T(128)S(1)}, s32[64]{0:T(128)}, u32[]{:S(2)}) copy-start(s32[64]{0:T(128)} %partner_any.1) | copy-start | bytes 772
  1.7 20.4 %all-to-all-start = ((f32[128,2,128]{2,1,0:T(2,128)}), f32[128,2,128]{2,1,0:T(2,128)S(1)}, u32[]{:S(2)}, u32[]{:S(2)}) async-start(f32[128,2,128]{2,1,0:T(2,128)} %bitcast.18), calls=%async_computation | async-start | bytes 262144 | tf_op jit(solution)/shard_map/all_to_all | solution.py:456
  14.6 13.5 %collective-permute-start = (f32[2,136,256]{2,1,0:T(8,128)S(1)}, f32[2,136,256]{2,1,0:T(8,128)S(1)}, u32[]{:S(2)}, u32[]{:S(2)}) collective-permute-start(f32[2,136,256]{2,1,0:T(8,128)S(1)} %get-tuple-element.13.sent_near), channel_id=1, source_target_pairs={{0,1},{1,0},{2,3},{3,2},{4,5},{5,4},{6,7},{7,6},{8,9},{9,8},{10,11... | collective-permute-start | bytes 835592 | tf_op jit(solution)/shard_map/ppermute | solution.py:461
  14.7 13.4 %collective-permute-start.1 = (f32[2,136,256]{2,1,0:T(8,128)S(1)}, f32[2,136,256]{2,1,0:T(8,128)S(1)}, u32[]{:S(2)}, u32[]{:S(2)}) collective-permute-start(f32[2,136,256]{2,1,0:T(8,128)S(1)} %get-tuple-element.14.sent_far), channel_id=1, source_target_pairs={{0,63},{1,2},{2,1},{3,4},{4,3},{5,6},{6,5},{7,8},{8,7},{9,10},{10,... | collective-permute-start | bytes 835592 | tf_op jit(solution)/shard_map/ppermute | solution.py:462
  22.1 6.0 %copy-start.1 = (f32[64,256]{1,0:T(8,128)S(1)}, f32[64,256]{1,0:T(8,128)}, u32[]{:S(2)}) copy-start(f32[64,256]{1,0:T(8,128)} %get-tuple-element.15.mask) | copy-start | bytes 196612
  22.1 6.0 %copy-start.2 = (f32[1,2,64]{2,1,0:T(2,128)S(1)}, f32[1,2,64]{2,1,0:T(2,128)}, u32[]{:S(2)}) copy-start(f32[1,2,64]{2,1,0:T(2,128)} %param.7) | copy-start | bytes 1540
  22.1 6.0 %copy-start.4 = (f32[1,2]{1,0:T(1,128)S(1)}, f32[1,2]{1,0:T(1,128)}, u32[]{:S(2)}) copy-start(f32[1,2]{1,0:T(1,128)} %param.8) | copy-start | bytes 28
  23.1 16.7 %all-to-all-start.1 = ((f32[128,2,128]{2,1,0:T(2,128)}), f32[128,2,128]{2,1,0:T(2,128)S(1)}, u32[]{:S(2)}, u32[]{:S(2)}) async-start(f32[128,2,128]{2,1,0:T(2,128)} %bitcast.6), calls=%async_computation.1 | async-start | bytes 262144 | tf_op jit(solution)/shard_map/all_to_all | solution.py:459

commit v7 on v6

--- a/solution.py
+++ b/solution.py
@@ -366,11 +366,12 @@
 
 
 def flux_kernel(chosen, got, back):
-    tiles, half = chosen.shape[0], got.shape[1]
+    tiles = chosen.shape[0]
     odd, even = pl.ds(1, tiles, stride=2), pl.ds(0, tiles, stride=2)
-    ocean = jnp.concatenate([got[pl.ds(2 * tiles + k, tiles, stride=2), :] for k in range(2)], 1)
+    ocean, wet = (got[pl.ds(2 * tiles + k, tiles, stride=2), :] for k in range(2))
     theirs = jnp.dot(chosen[...], ocean, precision=lax.Precision.HIGHEST, preferred_element_type=jnp.float32)
-    flux = got[odd, :] * (got[even, :] - theirs[:, 0:half]) * theirs[:, half:]
+    sea = jnp.dot(chosen[...], wet, preferred_element_type=jnp.float32)
+    flux = got[odd, :] * (got[even, :] - theirs) * sea
     turned = lax.dot_general(
         chosen[...], flux, (((0,), (0,)), ((), ())), precision=lax.Precision.HIGHEST, preferred_element_type=jnp.float32
     )
@@ -422,14 +423,19 @@
     d = ext[...]
     one0 = m * ((1.0 - 4.0 * h0 - v) * d + h0 * lateral(d))
     one1 = m * (v * d)
-    two0 = (1.0 - 4.0 * h0 - v) * one0 + h0 * lateral(one0) + v * one1
-    two1 = (1.0 - 4.0 * h1 - 2.0 * v) * one1 + h1 * lateral(one1) + v * one0
-    two2 = v * one1
-    for level, two in enumerate((two0, two1, two2)):
+    copies = []
+
+    def finish(level, two):
         three[level] = base[level] + (m * two)[8 : 8 + rows]
-    copy = pltpu.make_async_copy(three, out.at[0, pl.ds(0, 3)], sem)
-    copy.start()
-    copy.wait()
+        copy = pltpu.make_async_copy(three.at[level], out.at[0, level], sem.at[level])
+        copy.start()
+        copies.append(copy)
+
+    finish(2, v * one1)
+    finish(1, (1.0 - 4.0 * h1 - 2.0 * v) * one1 + h1 * lateral(one1) + v * one0)
+    finish(0, (1.0 - 4.0 * h0 - v) * one0 + h0 * lateral(one0) + v * one1)
+    for copy in copies:
+        copy.wait()
 
 
 def add_flux(base, back, mask, aux, whole):
@@ -441,7 +447,7 @@
         out_shape=jax.ShapeDtypeStruct(whole.shape, jnp.float32),
         in_specs=[vmem, vmem, vmem, vmem, hbm],
         out_specs=hbm,
-        scratch_shapes=[pltpu.VMEM((rows + 16, width), jnp.float32), pltpu.VMEM(base.shape, jnp.float32), pltpu.SemaphoreType.DMA],
+        scratch_shapes=[pltpu.VMEM((rows + 16, width), jnp.float32), pltpu.VMEM(base.shape, jnp.float32), pltpu.SemaphoreType.DMA((3,))],
         input_output_aliases={4: 0},
         compiler_params=pltpu.CompilerParams(vmem_limit_bytes=2 * MIB),
         cost_estimate=pl.CostEstimate(flops=30 * mask.size, bytes_accessed=32 * mask.size, transcendentals=0),

time: 41.4 us -> 41.3 us (level)
  no operation moved by 1% of the time
where the time goes in v7:
time: 41.3 us; the launch traced here: 40.7 us
  starting transfers between devices  23.6 us (57%)
  Pallas kernels  17 us (41%)
    pallas_call x1, Pallas kernels, mix(): pl.pallas_call(mix_kernel, out_shape=(jax.ShapeDtypeStruct(flat, jnp.floa...  11.7 us
    all_to_all x1, starting transfers between devices, per_device(): got = lax.all_to_all(outgoing, BOTH, 0, 0, tiled=True)  11.1 us
    ppermute x1, starting transfers between devices, per_device(): lax.ppermute(sent_far, 'tile', [(i, (i + 2 * (i % 2) - 1) % ntile) for i...  7.43 us
    all_to_all x1, starting transfers between devices, per_device(): back = lax.all_to_all(pieces, BOTH, 0, 0, tiled=True)  4.92 us
    pallas_call x1, Pallas kernels, edges(): pl.pallas_call(edge_kernel, out_shape=(shape, shape, jax.ShapeDtypeStruct...  1.71 us
    pallas_call x1, Pallas kernels, prep(): pl.pallas_call(prep_kernel, out_shape=(jax.ShapeDtypeStruct((4 * rows, wi...  1.65 us
    pallas_call x1, Pallas kernels, flux_pieces(): pl.pallas_call(flux_kernel, out_shape=jax.ShapeDtypeStruct(got.shape, jnp...  1.02 us
    pallas_call x1, Pallas kernels, add_flux(): pl.pallas_call(add_kernel, out_shape=jax.ShapeDtypeStruct(whole.shape, jn...  0.9 us
  transfers between devices with their start and end apart: 4, of which 0 were waited for; matrix products, arithmetic and copies ran while one was open for 0% of the time, Pallas kernels for 35%

profile of v7, /device:TPU:0, one launch (start us, length us, event | category | flops | bytes accessed | tf_op | source)
XLA Modules:
  0.0 40.7 jit_solution(12661127453505024809)
XLA Ops:
  0.0 0.0 copy-start
  0.0 0.0 copy-start.3
  0.0 1.7 %prep.1 = (f32[256,128]{1,0:T(8,128)}, f32[64,256]{1,0:T(8,128)}) custom-call(f32[2,64,64,256]{3,2,1,0:T(8,128)} %bitcast.14, f32[64,256]{1,0:T(8,128)} %coef_hbm.1, s32[64,256]{1,0:T(8,128)} %sea_hbm.1), custom_call_target="tpu_custom_call" | custom-call | flops 49152 | bytes 393216 | tf_op jit(solution)/shard_map/prep/pallas_call | solution.py:280
  1.7 11.1 %all-to-all-start = ((f32[128,2,128]{2,1,0:T(2,128)}), f32[128,2,128]{2,1,0:T(2,128)S(1)}, u32[]{:S(2)}, u32[]{:S(2)}) async-start(f32[128,2,128]{2,1,0:T(2,128)} %bitcast.18), calls=%async_computation | async-start | bytes 262144 | tf_op jit(solution)/shard_map/all_to_all | solution.py:462
  12.8 0.0 copy-done
  12.8 0.0 copy-done.3
  12.8 1.7 %edges.1 = (f32[2,136,256]{2,1,0:T(8,128)S(1)}, f32[2,136,256]{2,1,0:T(8,128)S(1)}, f32[64,64]{1,0:T(8,128)S(1)}) custom-call(f32[2,64,64,256]{3,2,1,0:T(8,128)} %bitcast.15, s32[64,256]{1,0:T(8,128)S(1)} %copy-done, s32[64]{0:T(128)S(1)} %copy-done.3), custom_call_target="tpu_custom_call" | custom-call | bytes 4194304 | tf_op jit(solution)/shard_map/edges/pallas_call | solution.py:351
  14.6 0.1 collective-permute-start
  14.7 7.4 %collective-permute-start.1 = (f32[2,136,256]{2,1,0:T(8,128)S(1)}, f32[2,136,256]{2,1,0:T(8,128)S(1)}, u32[]{:S(2)}, u32[]{:S(2)}) collective-permute-start(f32[2,136,256]{2,1,0:T(8,128)S(1)} %get-tuple-element.14.sent_far), channel_id=1, source_target_pairs={{0,63},{1,2},{2,1},{3,4},{4,3},{5,6},{6,5},{7,8},{8,7},{9,10},{10,... | collective-permute-start | bytes 835592 | tf_op jit(solution)/shard_map/ppermute | solution.py:468
  22.1 0.0 all-to-all-done
  22.1 0.0 copy-start.1
  22.1 0.0 copy-start.2
  22.1 0.0 copy-start.4
  22.1 1.0 %flux.1 = f32[256,128]{1,0:T(8,128)} custom-call(f32[64,64]{1,0:T(8,128)S(1)} %get-tuple-element.17.chosen, f32[256,128]{1,0:T(8,128)S(1)} %bitcast.11), custom_call_target="tpu_custom_call" | custom-call | flops 30000001024 | bytes 262144 | tf_op jit(solution)/shard_map/flux/pallas_call | solution.py:387
  23.1 4.9 %all-to-all-start.1 = ((f32[128,2,128]{2,1,0:T(2,128)}), f32[128,2,128]{2,1,0:T(2,128)S(1)}, u32[]{:S(2)}, u32[]{:S(2)}) async-start(f32[128,2,128]{2,1,0:T(2,128)} %bitcast.6), calls=%async_computation.1 | async-start | bytes 262144 | tf_op jit(solution)/shard_map/all_to_all | solution.py:465
  28.0 0.0 collective-permute-done.got_near
  28.0 0.0 collective-permute-done.1.got_far
  28.1 0.0 copy-done.1
  28.1 0.0 copy-done.2
  28.1 0.0 copy-done.4
  28.1 11.7 %mix.1 = (f32[128,64,256]{2,1,0:T(8,128)}, f32[3,64,256]{2,1,0:T(8,128)S(1)}, f32[8,256]{1,0:T(8,128)S(1)}) custom-call(f32[2,64]{1,0:T(2,128)S(1)} %bitcast.12, f32[2]{0:T(128)S(1)} %bitcast.13, f32[128,64,256]{2,1,0:T(8,128)} %bitcast.16, f32[2,136,256]{2,1,0:T(8,128)S(1)} %get-tuple-element.13.sent_near, f32[2,136,256]{2,1,0:T(8,128)S(1)} %get-tuple-element.14.sent_far, ...), custom_call_target="tpu_custom_call" | custom-call | flops 54525952 | bytes 16777216 | tf_op jit(solution)/shard_map/mix/pallas_call | solution.py:220
  39.8 0.0 all-to-all-done.1
  39.8 0.9 %add.1 = f32[2,64,64,256]{3,2,1,0:T(8,128)} custom-call(f32[3,64,256]{2,1,0:T(8,128)S(1)} %get-tuple-element.16.base, f32[256,128]{1,0:T(8,128)S(1)} %bitcast.10, f32[64,256]{1,0:T(8,128)S(1)} %copy-done.1, f32[8,256]{1,0:T(8,128)S(1)} %get-tuple-element.19.aux, f32[2,64,64,256]{3,2,1,0:T(8,128)} %bitcast.17), custom_call_target="tpu_custom_call", output_to_operand_aliasing={{}: (4, {})} | custom-call | flops 491520 | bytes 524288 | tf_op jit(solution)/shard_map/add/pallas_call | solution.py:445
Async XLA Ops:
  0.0 12.8 %copy-start = (s32[64,256]{1,0:T(8,128)S(1)}, s32[64,256]{1,0:T(8,128)}, u32[]{:S(2)}) copy-start(s32[64,256]{1,0:T(8,128)} %sea_hbm.1) | copy-start | bytes 196612
  0.0 12.8 %copy-start.3 = (s32[64]{0:T(128)S(1)}, s32[64]{0:T(128)}, u32[]{:S(2)}) copy-start(s32[64]{0:T(128)} %partner_any.1) | copy-start | bytes 772
  1.7 20.4 %all-to-all-start = ((f32[128,2,128]{2,1,0:T(2,128)}), f32[128,2,128]{2,1,0:T(2,128)S(1)}, u32[]{:S(2)}, u32[]{:S(2)}) async-start(f32[128,2,128]{2,1,0:T(2,128)} %bitcast.18), calls=%async_computation | async-start | bytes 262144 | tf_op jit(solution)/shard_map/all_to_all | solution.py:462
  14.6 13.5 %collective-permute-start = (f32[2,136,256]{2,1,0:T(8,128)S(1)}, f32[2,136,256]{2,1,0:T(8,128)S(1)}, u32[]{:S(2)}, u32[]{:S(2)}) collective-permute-start(f32[2,136,256]{2,1,0:T(8,128)S(1)} %get-tuple-element.13.sent_near), channel_id=1, source_target_pairs={{0,1},{1,0},{2,3},{3,2},{4,5},{5,4},{6,7},{7,6},{8,9},{9,8},{10,11... | collective-permute-start | bytes 835592 | tf_op jit(solution)/shard_map/ppermute | solution.py:467
  14.7 13.4 %collective-permute-start.1 = (f32[2,136,256]{2,1,0:T(8,128)S(1)}, f32[2,136,256]{2,1,0:T(8,128)S(1)}, u32[]{:S(2)}, u32[]{:S(2)}) collective-permute-start(f32[2,136,256]{2,1,0:T(8,128)S(1)} %get-tuple-element.14.sent_far), channel_id=1, source_target_pairs={{0,63},{1,2},{2,1},{3,4},{4,3},{5,6},{6,5},{7,8},{8,7},{9,10},{10,... | collective-permute-start | bytes 835592 | tf_op jit(solution)/shard_map/ppermute | solution.py:468
  22.1 6.0 %copy-start.1 = (f32[64,256]{1,0:T(8,128)S(1)}, f32[64,256]{1,0:T(8,128)}, u32[]{:S(2)}) copy-start(f32[64,256]{1,0:T(8,128)} %get-tuple-element.15.mask) | copy-start | bytes 196612
  22.1 6.0 %copy-start.2 = (f32[1,2,64]{2,1,0:T(2,128)S(1)}, f32[1,2,64]{2,1,0:T(2,128)}, u32[]{:S(2)}) copy-start(f32[1,2,64]{2,1,0:T(2,128)} %param.7) | copy-start | bytes 1540
  22.1 6.0 %copy-start.4 = (f32[1,2]{1,0:T(1,128)S(1)}, f32[1,2]{1,0:T(1,128)}, u32[]{:S(2)}) copy-start(f32[1,2]{1,0:T(1,128)} %param.8) | copy-start | bytes 28
  23.1 16.7 %all-to-all-start.1 = ((f32[128,2,128]{2,1,0:T(2,128)}), f32[128,2,128]{2,1,0:T(2,128)S(1)}, u32[]{:S(2)}, u32[]{:S(2)}) async-start(f32[128,2,128]{2,1,0:T(2,128)} %bitcast.6), calls=%async_computation.1 | async-start | bytes 262144 | tf_op jit(solution)/shard_map/all_to_all | solution.py:465
